TPU v7x, 32 devices: a whole 2x2x4 slice. The times are simulated.
32 devices in a mesh: width: 4 (over y, x), seq: 8 (over z, core).
Axes of the slice: x: 2, y: 2, z: 4, core: 2. Of those that a mesh axis runs over, the one named last changes fastest.
Arguments:
- activations: bfloat16 [8192, 28672], P('seq', 'width'), may hold values from -6 to 6
- errors: bfloat16 [8192, 8192], P('seq', 'width'), may hold values from -6 to 6
- proj_acts: bfloat16 [28672, 128], P('width'), may hold values from -0.03125 to 0.03125
- proj_errs: bfloat16 [8192, 128], P('width'), may hold values from -0.0625 to 0.0625
- fisher: float32 [16384, 16384], P('seq', 'width'), may hold values from -1 to 4, as said below
- queries: float32 [8, 2048, 128], P('seq', 'width'), may hold values from -6 to 6
Outputs:
- solution: float32 [8, 2048, 128], P('seq', 'width')
- residual: float32 [8, 2048, 128], P('seq', 'width')
- scores: float32 [128, 128], P(('width', 'seq'))
Inputs may be any that keep to these rules, and one draw needn't show every extreme that they name: `fisher`: symmetric and positive definite.
All inputs are finite; a program needn't handle non-finite values.
Results may differ from a plain program's by a relative error of at most 0.003.
Values may be sent and summed in bfloat16 or wider, within the bound.
No kernel may reach another device: no remote copies, remote signals or barrier semaphores. Data moves between devices by JAX's collectives and lax.ppermute only.
A program may use at most 192 MiB of HBM per device.

v0:
```python
import jax
import jax.numpy as jnp
from jax import lax
from jax.sharding import PartitionSpec as P

SEQ_LEN = 64


ridge_damp = 0.1
bound_low = 0.5
bound_high = 6.0


def chebyshev(apply_op, rhs):
    center = 0.5 * (bound_high + bound_low)
    half_width = 0.5 * (bound_high - bound_low)
    sigma_ratio = center / half_width
    rho_first = 1.0 / sigma_ratio
    rho_second = 1.0 / (2.0 * sigma_ratio - rho_first)
    step_one = rhs / center
    residue = rhs - apply_op(step_one)
    step_two = rho_second * rho_first * step_one + 2.0 * rho_second / half_width * residue
    iterate = step_one + step_two
    residue = residue - apply_op(step_two)
    return (iterate, residue)


def on_device(activations, errors, proj_acts, proj_errs, fisher, queries):
    highest = lax.Precision.HIGHEST
    width_count = lax.axis_size("width")
    seq_count = lax.axis_size("seq")
    width_rank = lax.axis_index("width")
    seq_rank = lax.axis_index("seq")
    proj_dim = proj_acts.shape[1]
    projected = lax.psum_scatter(
        jnp.concatenate(
            [
                jnp.dot(activations, proj_acts, preferred_element_type=jnp.float32),
                jnp.dot(errors, proj_errs, preferred_element_type=jnp.float32),
            ],
            axis=1,
        ),
        "width",
        scatter_dimension=0,
        tiled=True,
    )
    local_seqs = projected.shape[0] // SEQ_LEN
    act_proj = projected[:, :proj_dim].reshape(local_seqs, SEQ_LEN, proj_dim)
    err_proj = projected[:, proj_dim:].reshape(local_seqs, SEQ_LEN, proj_dim)
    seq_grads = jnp.einsum("sti,stk->sik", err_proj, act_proj, precision=highest) / SEQ_LEN
    seq_grads = seq_grads.reshape(local_seqs, proj_dim * proj_dim).astype(jnp.bfloat16)
    total_seqs = local_seqs * width_count * seq_count
    row_len = fisher.shape[0]
    col_len = fisher.shape[1]
    row_ids = seq_rank * row_len + lax.iota(jnp.int32, row_len)
    col_ids = width_rank * col_len + lax.iota(jnp.int32, col_len)
    base_tile = fisher + jnp.where(row_ids[:, None] == col_ids[None, :], ridge_damp, 0.0)
    contract = (((0,), (0,)), ((), ()))
    gathered = lax.all_gather(seq_grads, ("width", "seq"), axis=0, tiled=True)
    row_panel = lax.dynamic_slice_in_dim(gathered, seq_rank * row_len, row_len, 1)
    col_panel = lax.dynamic_slice_in_dim(gathered, width_rank * col_len, col_len, 1)
    damped = (
        base_tile
        + lax.dot_general(row_panel, col_panel, contract, preferred_element_type=jnp.float32)
        / total_seqs
    )
    piece_rows = queries.shape[1]
    query_count = queries.shape[2]
    group_ratio = seq_count // width_count

    def column_block(vector):
        strided = lax.all_gather(vector, "seq", axis=0, tiled=True)
        grouped = strided.reshape(width_count, group_ratio, 1, piece_rows, query_count)
        regrouped = lax.all_to_all(grouped, "width", split_axis=0, concat_axis=2, tiled=True)
        result = regrouped.reshape(col_len, query_count)
        return result

    def apply_op(vector):
        col_block = column_block(vector)
        return lax.psum_scatter(
            jnp.dot(damped, col_block, precision=highest, preferred_element_type=jnp.float32),
            "width",
            scatter_dimension=0,
            tiled=True,
        )

    rhs = queries.reshape(piece_rows, query_count)
    solution, residual = chebyshev(apply_op, rhs)
    own_grads = lax.dynamic_slice_in_dim(row_panel, width_rank * piece_rows, piece_rows, 1).astype(
        jnp.float32
    )
    partial_scores = jnp.dot(
        own_grads, solution, precision=highest, preferred_element_type=jnp.float32
    )
    partial_scores = partial_scores.reshape(width_count, seq_count, local_seqs, query_count)
    partial_scores = partial_scores.transpose(1, 0, 2, 3).reshape(total_seqs, query_count)
    scores = lax.psum_scatter(partial_scores, ("width", "seq"), scatter_dimension=0, tiled=True)
    return (
        solution.reshape(1, piece_rows, query_count),
        residual.reshape(1, piece_rows, query_count),
        scores,
    )


def solution(mesh):
    placed = (
        P("seq", "width"),
        P("seq", "width"),
        P("width", None),
        P("width", None),
        P("seq", "width"),
        P("seq", "width", None),
    )
    return jax.shard_map(
        on_device,
        mesh=mesh,
        in_specs=placed,
        out_specs=(P("seq", "width", None), P("seq", "width", None), P(("width", "seq"), None)),
        check_vma=False,
    )
```

profile of v0, /device:TPU:0, one launch (start us, length us, event | category | flops | bytes accessed | tf_op | source)
XLA Modules:
  0.0 390.7 jit_solution(4686555977368115952)
XLA Ops:
  8.0 0.0 copy-start
  8.0 0.0 reduce-scatter.4.cloned.1.call-start
  8.1 1.4 copy-done
  9.5 0.0 copy-start.3
  9.5 11.1 %fusion.11 = f32[1024,128]{0,1:T(8,128)} fusion(bf16[1024,7168]{1,0:T(8,128)(2,1)} %param.6, bf16[7168,128]{1,0:T(8,128)(2,1)S(1)} %copy-done), kind=kOutput, calls=%fused_computation.21 | convolution fusion | flops 1879048192 | bytes 17039360 | tf_op jit(solution)/shard_map/dot_general | solution.py:38
  20.6 0.0 copy-done.3
  20.6 0.0 copy-start.5
  20.6 0.0 copy-start.4
  20.6 2.6 fusion.12
  23.3 0.0 copy-done.5
  23.3 1.1 pad_maximum_fusion
  24.4 0.0 reduce-scatter.4.cloned.1.call-update
  24.4 0.0 all-gather.5.cloned.1.call-start
  24.4 0.0 copy-done.4
  24.5 0.7 bitcast_multiply_fusion.1
  25.2 0.0 all-gather.5.cloned.1.call-update
  25.2 0.0 all-gather.9.cloned.1.call-start
  25.3 29.7 %reduce-scatter.4.cloned.1.call-done = f32[256,256]{0,1:T(8,128)} async-done(((f32[1024,256]{0,1:T(8,128)}), f32[256,256]{0,1:T(8,128)}) %reduce-scatter.4.cloned.1.call-update) | async-done | bytes 262160 | tf_op jit(solution)/shard_map/reduce_scatter | solution.py:35
  55.0 1.0 fusion.10
  56.0 0.1 copy.18
  56.0 0.1 copy.17
  56.2 0.6 fusion
  56.8 0.7 reshape.62
  57.5 0.0 all-gather.9.cloned.1.call-update
  57.5 1.4 all-gather.5.cloned.1.call-done
  58.9 4.4 %all-to-all-start = ((f32[4,2,1,512,128]{4,3,1,2,0:T(8,128)}), f32[4,2,1,512,128]{4,3,1,2,0:T(8,128)}, u32[]{:S(2)}, u32[]{:S(2)}) async-start(f32[4,2,1,512,128]{4,3,1,2,0:T(8,128)} %bitcast.54), calls=%async_computation.1 | async-start | bytes 4194304 | tf_op jit(solution)/shard_map/all_to_all | solution.py:74
  63.4 0.2 reduce-scatter.6.cloned.1.call-start
  63.6 26.3 %all-to-all-done = f32[4,2,1,512,128]{4,3,1,2,0:T(8,128)} async-done(((f32[4,2,1,512,128]{4,3,1,2,0:T(8,128)}), f32[4,2,1,512,128]{4,3,1,2,0:T(8,128)}, u32[]{:S(2)}, u32[]{:S(2)}) %all-to-all-start) | async-done | bytes 2097184 | tf_op jit(solution)/shard_map/all_to_all | solution.py:74
  89.9 3.2 copy.20
  93.1 34.5 %all-gather.9.cloned.1.call-done = bf16[32,4,16384]{2,1,0:T(4,128)(2,1)} async-done(((bf16[1,4,16384]{2,1,0:T(4,128)(2,1)}), bf16[32,4,16384]{2,1,0:T(4,128)(2,1)}) %all-gather.9.cloned.1.call-update) | async-done | bytes 4194320 | tf_op jit(solution)/shard_map/all_gather | solution.py:59
  127.6 6.9 %reshape.63 = bf16[128,16384]{1,0:T(8,128)(2,1)} reshape(bf16[32,4,16384]{2,1,0:T(4,128)(2,1)} %all-gather.9.cloned.1.call-done) | data formatting | bytes 8388608
  134.5 0.0 copy-start.2
  134.5 22.8 %multiply_add_fusion = f32[2048,4096]{1,0:T(8,128)} fusion(f32[2048,4096]{1,0:T(8,128)} %param.10, s32[4096]{0:T(1024)S(1)} %iota_add_fusion, s32[2048]{0:T(1024)S(1)} %iota_add_fusion.1, bf16[128,16384]{1,0:T(8,128)(2,1)} %reshape.63, s32[]{:T(128)S(6)} %select_n.19, s32[]{:T(128)S(6)} %select_n.18), kind=kOutput, calls=%fused_computation | convolution fusion | flops 2189426688 | bytes 68706312 | tf_op jit(solution)/shard_map/dot_general | solution.py:64
  157.3 0.0 copy-done.2
  157.3 30.8 %fusion.13 = f32[2048,128]{1,0:T(8,128)} fusion(f32[2048,4096]{1,0:T(8,128)} %multiply_add_fusion, f32[4096,128]{1,0:T(8,128)S(1)} %bitcast.52), kind=kOutput, calls=%fused_computation.23 | convolution fusion | flops 12884901888 | bytes 36700160 | tf_op jit(solution)/shard_map/dot_general | solution.py:81
  188.2 0.0 reduce-scatter.6.cloned.1.call-update
  188.2 0.0 all-gather.7.cloned.1.call-start
  188.2 26.6 %reduce-scatter.6.cloned.1.call-done = f32[512,128]{1,0:T(8,128)} async-done(((f32[2048,128]{1,0:T(8,128)}), f32[512,128]{1,0:T(8,128)}) %reduce-scatter.6.cloned.1.call-update) | async-done | bytes 262160 | tf_op jit(solution)/shard_map/reduce_scatter | solution.py:80
  214.8 1.8 add_bitcast_fusion
  216.6 0.0 copy-start.6
  216.6 0.0 all-gather.7.cloned.1.call-update
  216.6 29.1 %all-gather.7.cloned.1.call-done = f32[4096,128]{1,0:T(8,128)} async-done(((f32[512,128]{1,0:T(8,128)}), f32[4096,128]{1,0:T(8,128)}) %all-gather.7.cloned.1.call-update) | async-done | bytes 2097168 | tf_op jit(solution)/shard_map/all_gather | solution.py:72
  245.8 4.4 %all-to-all-start.1 = ((f32[4,2,1,512,128]{4,3,1,2,0:T(8,128)}), f32[4,2,1,512,128]{4,3,1,2,0:T(8,128)}, u32[]{:S(2)}, u32[]{:S(2)}) async-start(f32[4,2,1,512,128]{4,3,1,2,0:T(8,128)} %bitcast.55), calls=%async_computation.3 | async-start | bytes 4194304 | tf_op jit(solution)/shard_map/all_to_all | solution.py:74
  250.2 0.0 all-reduce.3.cloned.1.call-start
  250.3 0.0 copy-done.6
  250.3 1.3 fusion.4
  251.6 0.6 copy.23
  252.2 0.0 all-reduce.3.cloned.1.call-update
  252.2 0.3 reduce-scatter.8.cloned.1.call-start
  252.5 23.5 %all-to-all-done.1 = f32[4,2,1,512,128]{4,3,1,2,0:T(8,128)} async-done(((f32[4,2,1,512,128]{4,3,1,2,0:T(8,128)}), f32[4,2,1,512,128]{4,3,1,2,0:T(8,128)}, u32[]{:S(2)}, u32[]{:S(2)}) %all-to-all-start.1) | async-done | bytes 2097184 | tf_op jit(solution)/shard_map/all_to_all | solution.py:74
  276.0 1.7 copy.22
  277.8 0.0 copy-start.7
  277.8 0.0 copy-start.1
  277.8 31.1 %fusion.14 = f32[2048,128]{1,0:T(8,128)} fusion(f32[2048,4096]{1,0:T(8,128)} %multiply_add_fusion, f32[4096,128]{1,0:T(8,128)S(1)} %bitcast.53), kind=kOutput, calls=%fused_computation.24 | convolution fusion | flops 12884901888 | bytes 36700160 | tf_op jit(solution)/shard_map/dot_general | solution.py:81
  308.9 0.0 reduce-scatter.8.cloned.1.call-update
  308.9 71.5 %all-reduce.3.cloned.1.call-done = f32[128,128]{1,0:T(8,128)} async-done(((f32[128,128]{1,0:T(8,128)}), f32[128,128]{1,0:T(8,128)}) %all-reduce.3.cloned.1.call-update) | async-done | bytes 65552
  380.3 1.3 constant_dynamic-slice_fusion
  381.6 0.0 reduce-scatter.8.cloned.1.call-done
  381.6 0.0 copy-done.7
  381.6 1.7 subtract_bitcast_fusion
  383.3 0.0 copy-done.1
  (2 shorter events, 0.0 us)
Async XLA Ops:
  8.0 1.5 copy-start
  8.0 47.0 %reduce-scatter.4.cloned.1.call-start = ((), (), s32[]{:S(2)}) async-start(), calls=%async_computation.5 | async-start | bytes 1310720 | tf_op jit(solution)/shard_map/reduce_scatter | solution.py:35
  9.5 11.1 %copy-start.3 = (bf16[1024,2048]{1,0:T(8,128)(2,1)S(1)}, bf16[1024,2048]{1,0:T(8,128)(2,1)}, u32[]{:S(2)}) copy-start(bf16[1024,2048]{1,0:T(8,128)(2,1)} %param.7) | copy-start | bytes 12582916
  20.6 2.6 copy-start.5
  20.6 3.8 copy-start.4
  24.4 34.5 %all-gather.5.cloned.1.call-start = ((), (), s32[]{:S(2)}) async-start(), calls=%async_computation.6 | async-start | bytes 2359296 | tf_op jit(solution)/shard_map/all_gather | solution.py:72
  25.2 102.4 %all-gather.9.cloned.1.call-start = ((), (), s32[]{:S(2)}) async-start(), calls=%async_computation.10 | async-start | bytes 4325376 | tf_op jit(solution)/shard_map/all_gather | solution.py:59
  58.9 31.0 %all-to-all-start = ((f32[4,2,1,512,128]{4,3,1,2,0:T(8,128)}), f32[4,2,1,512,128]{4,3,1,2,0:T(8,128)}, u32[]{:S(2)}, u32[]{:S(2)}) async-start(f32[4,2,1,512,128]{4,3,1,2,0:T(8,128)} %bitcast.54), calls=%async_computation.1 | async-start | bytes 4194304 | tf_op jit(solution)/shard_map/all_to_all | solution.py:74
  63.4 151.4 %reduce-scatter.6.cloned.1.call-start = ((), (), s32[]{:S(2)}) async-start(), calls=%async_computation.7 | async-start | bytes 1310720 | tf_op jit(solution)/shard_map/reduce_scatter | solution.py:80
  134.5 22.8 %copy-start.2 = (f32[4,2,1,512,128]{4,3,0,1,2:T(8,128)S(1)}, f32[4,2,1,512,128]{4,3,0,1,2:T(8,128)}, u32[]{:S(2)}) copy-start(f32[4,2,1,512,128]{4,3,0,1,2:T(8,128)} %copy.20) | copy-start | bytes 6291460
  188.2 57.6 %all-gather.7.cloned.1.call-start = ((), (), s32[]{:S(2)}) async-start(), calls=%async_computation.8 | async-start | bytes 2359296 | tf_op jit(solution)/shard_map/all_gather | solution.py:72
  216.6 33.7 %copy-start.6 = (f32[512,128]{1,0:T(8,128)S(1)}, f32[512,128]{1,0:T(8,128)}, u32[]{:S(2)}) copy-start(f32[512,128]{1,0:T(8,128)} %get-tuple-element.4) | copy-start | bytes 786436
  245.8 30.2 %all-to-all-start.1 = ((f32[4,2,1,512,128]{4,3,1,2,0:T(8,128)}), f32[4,2,1,512,128]{4,3,1,2,0:T(8,128)}, u32[]{:S(2)}, u32[]{:S(2)}) async-start(f32[4,2,1,512,128]{4,3,1,2,0:T(8,128)} %bitcast.55), calls=%async_computation.3 | async-start | bytes 4194304 | tf_op jit(solution)/shard_map/all_to_all | solution.py:74
  250.2 130.1 %all-reduce.3.cloned.1.call-start = ((), (), s32[]{:S(2)}) async-start(), calls=%async_computation.11 | async-start | bytes 131072
  252.2 129.4 %reduce-scatter.8.cloned.1.call-start = ((), (), s32[]{:S(2)}) async-start(), calls=%async_computation.9 | async-start | bytes 1310720 | tf_op jit(solution)/shard_map/reduce_scatter | solution.py:80
  277.8 103.8 %copy-start.7 = (f32[512,128]{1,0:T(8,128)S(1)}, f32[512,128]{1,0:T(8,128)}, u32[]{:S(2)}) copy-start(f32[512,128]{1,0:T(8,128)} %reduce-scatter.6.cloned.1.call-done) | copy-start | bytes 786436
  277.8 105.5 %copy-start.1 = (bf16[7168,128]{1,0:T(8,128)(2,1)S(1)}, bf16[7168,128]{1,0:T(8,128)(2,1)}, u32[]{:S(2)}) copy-start(bf16[7168,128]{1,0:T(8,128)(2,1)} %param.8) | copy-start | bytes 5505028
Sparse Core Ops, SparseCore 0:
  24.5 30.4 reduce-scatter.3
  188.3 26.4 reduce-scatter.5
  309.0 26.2 reduce-scatter.7
Sparse Core Ops, SparseCore 1:
  27.1 31.7 all-gather.4
  62.8 64.8 all-gather.8
  216.7 29.0 all-gather.6
  258.1 122.2 all-reduce.2
where the time goes:
time: 393 us; the launch traced here: 391 us
  waiting for transfers between devices  243 us (62%)
  matrix products  100 us (25%)
  local copies, waits for them, and re-layouts  17.1 us (4%)
  between operations  15.6 us (4%)
  starting transfers between devices  9.59 us (2%)
  other arithmetic  5.35 us (1%)
    unnamed x8, waiting for transfers between devices  71.6 us
    dot_general x2, matrix products, apply_op(): jnp.dot(damped, col_block, precision=highest, preferred_element_type=jnp....  61.9 us
    all_to_all x2, waiting for transfers between devices, column_block(): lax.all_to_all(grouped, 'width', split_axis=0, concat_axis=2, tiled=True)  49.8 us
    all_gather x1, waiting for transfers between devices, on_device(): gathered = lax.all_gather(seq_grads, ('width', 'seq'), axis=0, tiled=True)  34.5 us
    all_gather x2, waiting for transfers between devices, column_block(): strided = lax.all_gather(vector, 'seq', axis=0, tiled=True)  30.6 us
    reduce_scatter x1, waiting for transfers between devices, on_device(): lax.psum_scatter(jnp.concatenate([jnp.dot(activations, proj_acts, preferr...  29.7 us
    reduce_scatter x2, waiting for transfers between devices, apply_op(): lax.psum_scatter(jnp.dot(damped, col_block, precision=highest, preferred_...  26.6 us
    dot_general x1, matrix products, on_device(): lax.dot_general(row_panel, col_panel, contract, preferred_element_type=jn...  22.8 us
  transfers between devices with their start and end apart: 9, of which 8 were waited for; matrix products, arithmetic and copies ran while one was open for 11% of the time, Pallas kernels for 0%

commit v1 on v0

v1 whole, which is shorter than its diff:
```python
import jax
import jax.numpy as jnp
from jax import lax
from jax.experimental import pallas as pl
from jax.experimental.pallas import tpu as pltpu
from jax.sharding import PartitionSpec as P

SEQ_LEN = 64

ridge_damp = 0.1
bound_low = 0.5
bound_high = 6.0
center = 0.5 * (bound_high + bound_low)
half_width = 0.5 * (bound_high - bound_low)
rho_first = half_width / center
rho_second = 1.0 / (2.0 * center / half_width - rho_first)
fall = rho_second * rho_first
lead = (1.0 + fall) / center
tail = 2.0 * rho_second / half_width / center

BF16 = jnp.bfloat16
F32 = jnp.float32
HIGHEST = lax.Precision.HIGHEST
MIB = 1024 * 1024
NN = (((1,), (0,)), ((), ()))
NT = (((1,), (1,)), ((), ()))
TN = (((0,), (0,)), ((), ()))

WHOLE = pl.BlockSpec(memory_space=pltpu.VMEM)
SCALARS = pl.BlockSpec(memory_space=pltpu.SMEM)


def shaped(shape, dtype):
    return jax.ShapeDtypeStruct(shape, dtype)


def dot(a, b, dims, precision=None):
    return lax.dot_general(a, b, dims, precision=precision, preferred_element_type=F32)


def swap(x, axis, k):
    return lax.ppermute(x, axis, [(i, i ^ k) for i in range(lax.axis_size(axis))])


def call(body, out, args, flops=0, limit=32, **kw):
    moved = sum(a.size * a.dtype.itemsize for a in args)
    return pl.pallas_call(
        body,
        out_shape=out,
        compiler_params=pltpu.CompilerParams(vmem_limit_bytes=limit * MIB),
        cost_estimate=pl.CostEstimate(flops=flops, bytes_accessed=moved, transcendentals=0),
        **kw,
    )(*args)


def project(ranks, activations, errors, proj_acts, proj_errs, n_w):
    tokens, feats_a = activations.shape
    feats_e = errors.shape[1]
    rank = proj_acts.shape[1]
    own = tokens // n_w
    rows = min(128, own)
    per = own // rows

    def body(ranks_ref, act_ref, err_ref, pa_ref, pe_ref, *outs):
        step = pl.program_id(0)
        a = dot(act_ref[...], pa_ref[...], NN)
        e = dot(err_ref[...], pe_ref[...], NN)
        at = pl.multiple_of((step % per) * rows, rows)
        for r in range(n_w):

            @pl.when(step // per == r)
            def _():
                outs[r][pl.ds(at, rows), :rank] = a
                outs[r][pl.ds(at, rows), rank:] = e

    block = lambda i, ranks: ((ranks[0] ^ (i // per)) * per + i % per, 0)
    keep = lambda i, ranks: (0, 0)
    return pl.pallas_call(
        body,
        out_shape=[shaped((own, 2 * rank), F32)] * n_w,
        grid_spec=pltpu.PrefetchScalarGridSpec(
            num_scalar_prefetch=1,
            grid=(n_w * per,),
            in_specs=[
                pl.BlockSpec((rows, feats_a), block),
                pl.BlockSpec((rows, feats_e), block),
                pl.BlockSpec((feats_a, rank), keep),
                pl.BlockSpec((feats_e, rank), keep),
            ],
            out_specs=[pl.BlockSpec((own, 2 * rank), keep)] * n_w,
        ),
        compiler_params=pltpu.CompilerParams(vmem_limit_bytes=32 * MIB),
        cost_estimate=pl.CostEstimate(
            flops=2 * tokens * (feats_a + feats_e) * rank,
            bytes_accessed=2 * tokens * (feats_a + feats_e),
            transcendentals=0,
        ),
    )(ranks, activations, errors, proj_acts, proj_errs)


def gradients(parts):
    tokens, both = parts[0].shape
    rank = both // 2
    seqs = tokens // SEQ_LEN

    def body(*refs):
        ins, out = refs[:-1], refs[-1]
        total = ins[0][...]
        for ref in ins[1:]:
            total = total + ref[...]
        for j in range(seqs):
            rows = slice(j * SEQ_LEN, (j + 1) * SEQ_LEN)
            g = dot(total[rows, rank:], total[rows, :rank], TN, HIGHEST)
            out[j] = (g / SEQ_LEN).astype(BF16)

    return call(body, shaped((seqs, rank, rank), BF16), parts)


def first_product(ranks, fisher, rhs_t, n_w, n_s, parity):
    row_len, col_len = fisher.shape
    chunk = col_len // n_s
    count = rhs_t[0].shape[0]
    steps = n_s // 2
    width = min(256, chunk)
    sub = chunk // width
    shift = ridge_damp - center

    def body(ranks_ref, fisher_ref, *refs):
        vec, (y_ref, keep_ref) = refs[:n_w], refs[n_w:]
        t = pl.program_id(0) // sub
        h = pl.program_id(0) % sub
        w, s = ranks_ref[0], ranks_ref[1]
        p = 2 * t + parity
        cols = pl.ds(pl.multiple_of(h * width, width), width)
        total = jnp.zeros((count, width), F32)
        for r in range(n_w):
            rows = pl.ds(pl.multiple_of((w ^ r) * chunk, chunk), chunk)
            keep_ref[t, r, :, cols] = fisher_ref[rows, :].astype(BF16)

            @pl.when(w * n_s + (s ^ p) == s * n_w + (w ^ r))
            def _():
                i = lax.broadcasted_iota(jnp.int32, (chunk, width), 0)
                j = lax.broadcasted_iota(jnp.int32, (chunk, width), 1) + h * width
                block = fisher_ref[rows, :]
                keep_ref[t, r, :, cols] = (block + jnp.where(i == j, shift, 0.0)).astype(BF16)

            total = total + dot(vec[r][...], keep_ref[t, r, :, cols], NN)
        y_ref[t, :, cols] = total

    column = lambda i, ranks: (0, (ranks[1] ^ (2 * (i // sub) + parity)) * sub + i % sub)
    return pl.pallas_call(
        body,
        out_shape=[
            shaped((steps, count, chunk), F32),
            pltpu.VMEM((steps, n_w, chunk, chunk), BF16),
        ],
        grid_spec=pltpu.PrefetchScalarGridSpec(
            num_scalar_prefetch=1,
            grid=(steps * sub,),
            in_specs=[pl.BlockSpec((row_len, width), column)] + [WHOLE] * n_w,
            out_specs=[WHOLE, WHOLE],
        ),
        compiler_params=pltpu.CompilerParams(vmem_limit_bytes=24 * MIB),
        cost_estimate=pl.CostEstimate(
            flops=row_len * col_len * count,
            bytes_accessed=2 * row_len * col_len,
            transcendentals=0,
        ),
    )(ranks, fisher, *rhs_t)


def fold_cores(mine, theirs):
    steps, count, chunk = mine.shape

    def body(mine_ref, theirs_ref, own_ref, *outs):
        own_ref[...] = mine_ref[0] + theirs_ref[0]
        for t in range(1, steps):
            outs[t - 1][...] = (mine_ref[t] + theirs_ref[t]).astype(BF16)

    outs = [shaped((count, chunk), F32)] + [shaped((count, chunk), BF16)] * (steps - 1)
    return call(body, outs, [mine, theirs])


def fold_chips(own, others):
    def body(*refs):
        total = refs[0][...]
        for ref in refs[1:-1]:
            total = total + ref[...].astype(F32)
        refs[-1][...] = total.astype(BF16)

    return call(body, shaped(own.shape, BF16), [own, *others])


def panel(ranks, near, far, q_near, q_far, n_s):
    lines, group, rank = near[0].shape
    steps = len(near)
    seqs = n_s * group
    count, chunk = q_near[0].shape
    per = chunk // rank

    def body(ranks_ref, *refs):
        near_refs, far_ref = refs[:steps], refs[steps]
        q_refs, q_far_ref = refs[steps + 1 : 2 * steps + 1], refs[2 * steps + 1]
        g_ref, gq_ref = refs[2 * steps + 2 :]
        s = ranks_ref[1]
        total = jnp.zeros((seqs, count), F32)
        for p in range(n_s):
            for ii in range(per):
                line = (s ^ p) * per + ii
                for j in range(n_s):
                    piece = near_refs[j // 2][line] if j % 2 == 0 else far_ref[j // 2, line]
                    g_ref[p, j * group : (j + 1) * group, ii * rank : (ii + 1) * rank] = piece
            q = q_refs[p // 2][...] if p % 2 == 0 else q_far_ref[p // 2]
            total = total + dot(g_ref[p], q, NT)
        gq_ref[...] = total

    args = [ranks, *near, far, *q_near, q_far]
    return call(
        body,
        [shaped((n_s, seqs, chunk), BF16), shaped((seqs, count), F32)],
        args,
        in_specs=[SCALARS] + [WHOLE] * (len(args) - 1),
        out_specs=[WHOLE, WHOLE],
    )


def second_product(keep_even, keep_odd, y_near, y_far, grads):
    steps, n_w, chunk, _ = keep_even.shape
    n_s, seqs, _ = grads.shape
    count = y_near[0].shape[0]

    def body(even_ref, odd_ref, *refs):
        y_refs, y_far_ref, g_ref = refs[:steps], refs[steps], refs[steps + 1]
        tile_ref, small_ref, x_ref = refs[steps + 2 :]
        small = jnp.zeros((seqs, count + seqs), F32)
        for p in range(n_s):
            x_ref[p, :count] = y_refs[p // 2][...] if p % 2 == 0 else y_far_ref[p // 2]
            x_ref[p, count:] = g_ref[p]
            small = small + dot(g_ref[p], x_ref[p], NT)
        small_ref[...] = small

        def one(r, carry):
            total = jnp.zeros((chunk, count + seqs), F32)
            for p in range(n_s):
                block = even_ref[p // 2, r] if p % 2 == 0 else odd_ref[p // 2, r]
                total = total + dot(block, x_ref[p], NT)
            tile_ref[r] = total
            return carry

        lax.fori_loop(0, n_w, one, 0)

    args = [keep_even, keep_odd, *y_near, y_far, grads]
    return call(
        body,
        [shaped((n_w, chunk, count + seqs), F32), shaped((seqs, count + seqs), F32)],
        args,
        flops=2 * n_w * chunk * chunk * n_s * (count + seqs),
        in_specs=[WHOLE] * len(args),
        out_specs=[WHOLE, WHOLE],
        scratch_shapes=[pltpu.VMEM((n_s, count + seqs, chunk), BF16)],
    )


def combine(tile, small, first):
    n_w, chunk, both = tile.shape
    seqs, count = first.shape

    def body(tile_ref, small_ref, first_ref, own_ref, *outs):
        u = first_ref[...]
        for r in range(n_w):
            part = tile_ref[r, :, :count] + dot(tile_ref[r, :, count:], u, NN, HIGHEST)
            if r == 0:
                own_ref[...] = part
            else:
                outs[r - 1][...] = part.astype(BF16)
        outs[n_w - 1][...] = small_ref[:, :count] + dot(small_ref[:, count:], u, NN, HIGHEST)

    outs = [shaped((chunk, count), F32)] + [shaped((chunk, count), BF16)] * (n_w - 1)
    return call(body, outs + [shaped((seqs, count), F32)], [tile, small, first])


def finish(ranks, rhs, y_own, g_own, first, seconds, parts, n_w, n_s):
    chunk, count = rhs.shape
    seqs = first.shape[0]
    group = seqs // n_s
    local = seqs // (n_w * n_s)

    def body(ranks_ref, rhs_ref, y_ref, g_ref, first_ref, *refs):
        second_refs, part_refs = refs[:n_w], refs[n_w : 2 * n_w]
        sol_ref, res_ref, score_ref, coef_ref, order_ref = refs[2 * n_w :]
        w, s = ranks_ref[0], ranks_ref[1]
        source = (s * n_w + w) % n_s
        for p in range(n_s):
            rows = pl.ds(pl.multiple_of((source ^ s ^ p) * group, group), group)
            order_ref[p * group : (p + 1) * group, :] = g_ref[rows, :].astype(F32)
        first = first_ref[...]
        second = second_refs[0][...]
        for ref in second_refs[1:]:
            second = second + ref[...]
        second = second / seqs
        q = rhs_ref[...]
        g = order_ref[...]
        once = y_ref[...].astype(F32).T + dot(g, first, TN, HIGHEST)
        twice = part_refs[0][...] + dot(g, second, TN, HIGHEST)
        for ref in part_refs[1:]:
            twice = twice + ref[...].astype(F32)
        sol_ref[...] = lead * q - tail * once
        res_ref[...] = tail * twice - fall * q
        coef_ref[...] = seqs * (lead * first - tail * second)
        for j in range(local):
            row = (w * n_s + s) * local + j
            at = ((row // group) ^ s) * group + row % group
            score_ref[pl.ds(j, 1), :] = coef_ref[pl.ds(at, 1), :]

    args = [ranks, rhs, y_own, g_own, first, *seconds, *parts]
    return call(
        body,
        [shaped((chunk, count), F32), shaped((chunk, count), F32), shaped((local, count), F32)],
        args,
        in_specs=[SCALARS] + [WHOLE] * (len(args) - 1),
        out_specs=[WHOLE] * 3,
        scratch_shapes=[pltpu.VMEM((seqs, count), F32), pltpu.VMEM((seqs, chunk), F32)],
    )


def on_device(activations, errors, proj_acts, proj_errs, fisher, queries):
    n_w = lax.axis_size("width")
    n_s = lax.axis_size("seq")
    steps = n_s // 2
    ranks = jnp.stack([lax.axis_index("width"), lax.axis_index("seq")]).astype(jnp.int32)
    rank = proj_acts.shape[1]
    rhs = queries.reshape(queries.shape[1:])
    both = ("width", "seq")
    to_columns = []
    for block in range(n_w * n_s):
        by_row = (block % n_w) * n_s + block // n_w
        to_columns.append((by_row, block))
    to_rows = [(b, a) for a, b in to_columns]

    rhs_t = rhs.T.astype(BF16)
    rows_t = [rhs_t] + [swap(rhs_t, "width", r) for r in range(1, n_w)]
    q_cols = lax.ppermute(rhs_t, both, to_columns)
    q_near = [q_cols] + [swap(q_cols, "seq", 2 * t) for t in range(1, steps)]
    q_far = swap(jnp.stack(q_near), "seq", 1)

    pieces = project(ranks, activations, errors, proj_acts, proj_errs, n_w)
    pieces = [pieces[0]] + [swap(pieces[r], "width", r) for r in range(1, n_w)]
    grads = gradients(pieces)
    local = grads.shape[0]
    lines = rank // n_w
    split = grads.reshape(local, n_w, lines, rank).transpose(1, 0, 2, 3)
    split = lax.all_to_all(split, "width", split_axis=0, concat_axis=0, tiled=True)
    group = n_w * local
    near = split.reshape(group, lines, rank).transpose(1, 0, 2)
    near = [near] + [swap(near, "seq", 2 * t) for t in range(1, steps)]
    far = swap(jnp.stack(near), "seq", 1)
    grads, first = panel(ranks, near, far, q_near, q_far, n_s)
    g_own = lax.ppermute(grads[0], both, to_rows)
    seqs = first.shape[0]

    theirs, keep_odd = first_product(ranks, fisher, rows_t, n_w, n_s, 1)
    theirs = swap(theirs, "seq", 1)
    mine, keep_even = first_product(ranks, fisher, rows_t, n_w, n_s, 0)
    own, *sent = fold_cores(mine, theirs)
    y = fold_chips(own, [swap(sent[t - 1], "seq", 2 * t) for t in range(1, steps)])
    y_own = lax.ppermute(y, both, to_rows)
    y_near = [y] + [swap(y, "seq", 2 * t) for t in range(1, steps)]
    y_far = swap(jnp.stack(y_near), "seq", 1)

    first = sum([swap(first, "width", r) for r in range(1, n_w)], first) / seqs
    tile, small = second_product(keep_even, keep_odd, y_near, y_far, grads)
    own, *sent, second = combine(tile, small, first)
    parts = [own] + [swap(sent[r - 1], "width", r) for r in range(1, n_w)]
    seconds = [second] + [swap(second, "width", r) for r in range(1, n_w)]
    solution, residual, scores = finish(
        ranks, rhs, y_own, g_own, first, seconds, parts, n_w, n_s
    )
    return solution.reshape(queries.shape), residual.reshape(queries.shape), scores


def solution(mesh):
    placed = (
        P("seq", "width"),
        P("seq", "width"),
        P("width", None),
        P("width", None),
        P("seq", "width"),
        P("seq", "width", None),
    )
    return jax.shard_map(
        on_device,
        mesh=mesh,
        in_specs=placed,
        out_specs=(P("seq", "width", None), P("seq", "width", None), P(("width", "seq"), None)),
        check_vma=False,
    )
```

time: 393 us -> 174 us (0.44)
  waiting for transfers between devices: 243 us -> 40.6 us
  matrix products: 100 us -> 0 us
  starting transfers between devices: 9.59 us -> 57 us
  Pallas kernels: 0 us -> 40 us
  between operations: 15.6 us -> 0.97 us
  blocking collectives: 0 us -> 10.5 us
    dot_general x7 -> x0, matrix products: 100 us -> none  [the longest x2 61.9 us: apply_op(): jnp.dot(damped, col_block, precision=highest, preferred_element_type=jnp....]
    unnamed x8 -> x0, waiting for transfers between devices: 71.6 us -> none
    all_gather x3 -> x0, waiting for transfers between devices: 65.1 us -> none  [the longest x1 34.5 us: on_device(): gathered = lax.all_gather(seq_grads, ('width', 'seq'), axis=0, tiled=True)]
    ppermute x0 -> x34, starting transfers between devices: none -> 57 us  [the longest x31 55 us: swap(): lax.ppermute(x, axis, [(i, i ^ k) for i in range(lax.axis_size(axis))])]
    reduce_scatter x3 -> x0, waiting for transfers between devices: 56.3 us -> none  [the longest x1 29.7 us: on_device(): lax.psum_scatter(jnp.concatenate([jnp.dot(activations, proj_acts, preferr...]
    all_to_all x2 -> x0, waiting for transfers between devices: 49.8 us -> none  [column_block(): lax.all_to_all(grouped, 'width', split_axis=0, concat_axis=2, tiled=True)]
    ppermute x0 -> x34, waiting for transfers between devices: none -> 40.6 us  [the longest x31 40.6 us: swap(): lax.ppermute(x, axis, [(i, i ^ k) for i in range(lax.axis_size(axis))])]
    pallas_call x0 -> x10, Pallas kernels: none -> 40 us  [the longest x2 22.5 us: first_product(): pl.pallas_call(body, out_shape=[shaped((steps, count, chunk), F32), pltpu...]
  transfers between devices with their start and end apart: 9 -> 34, of which waited for: 8 -> 12; matrix products, arithmetic and copies ran while one was open for 11% -> 3% of each run, Pallas kernels for 0% -> 15%
where the time goes in v1:
time: 174 us; the launch traced here: 173 us
  starting transfers between devices  57 us (33%)
  waiting for transfers between devices  40.6 us (23%)
  Pallas kernels  40 us (23%)
  local copies, waits for them, and re-layouts  20.8 us (12%)
  blocking collectives  10.5 us (6%)
  other arithmetic  3.69 us (2%)
    ppermute x31, starting transfers between devices, swap(): lax.ppermute(x, axis, [(i, i ^ k) for i in range(lax.axis_size(axis))])  55 us
    ppermute x31, waiting for transfers between devices, swap(): lax.ppermute(x, axis, [(i, i ^ k) for i in range(lax.axis_size(axis))])  40.6 us
    pallas_call x2, Pallas kernels, first_product(): pl.pallas_call(body, out_shape=[shaped((steps, count, chunk), F32), pltpu...  22.5 us
    unnamed x18, local copies, waits for them, and re-layouts  18.5 us
    pallas_call x7, Pallas kernels, call(): pl.pallas_call(body, out_shape=out, compiler_params=pltpu.CompilerParams(...  10.6 us
    all_to_all x1, blocking collectives, on_device(): lax.all_to_all(split, 'width', split_axis=0, concat_axis=0, tiled=True)  10.5 us
    pallas_call x1, Pallas kernels, project(): pl.pallas_call(body, out_shape=[shaped((own, 2 * rank), F32)] * n_w, grid...  6.86 us
  transfers between devices with their start and end apart: 34, of which 12 were waited for; matrix products, arithmetic and copies ran while one was open for 3% of the time, Pallas kernels for 15%

profile of v1, /device:TPU:0, one launch (start us, length us, event | category | flops | bytes accessed | tf_op | source)
XLA Modules:
  0.0 173.5 jit_solution(9787354103092438374)
XLA Ops:
  0.6 1.0 convert_bitcast_fusion
  1.6 3.0 %collective-permute-start = (bf16[128,512]{0,1:T(8,128)(2,1)S(1)}, bf16[128,512]{0,1:T(8,128)(2,1)S(1)}, u32[]{:S(2)}, u32[]{:S(2)}) collective-permute-start(bf16[128,512]{0,1:T(8,128)(2,1)S(1)} %convert_bitcast_fusion), channel_id=1, source_target_pairs={{0,8},{8,0},{16,24},{24,16},{1,9},{9,1},{17,25},{25,17},{2,10},{10... | collective-permute-start | bytes 393224 | tf_op jit(solution)/shard_map/ppermute | solution.py:42
  4.6 1.5 collective-permute-start.1
  6.1 0.1 copy.23.refs_0_
  6.3 2.2 %collective-permute-done = bf16[128,512]{0,1:T(8,128)(2,1)S(1)} collective-permute-done((bf16[128,512]{0,1:T(8,128)(2,1)S(1)}, bf16[128,512]{0,1:T(8,128)(2,1)S(1)}, u32[]{:S(2)}, u32[]{:S(2)}) %collective-permute-start) | collective-permute-done | bytes 131104 | tf_op jit(solution)/shard_map/ppermute | solution.py:42
  8.6 3.8 %collective-permute-done.1 = bf16[128,512]{0,1:T(8,128)(2,1)S(1)} collective-permute-done((bf16[128,512]{0,1:T(8,128)(2,1)S(1)}, bf16[128,512]{0,1:T(8,128)(2,1)S(1)}, u32[]{:S(2)}, u32[]{:S(2)}) %collective-permute-start.1) | collective-permute-done | bytes 131104 | tf_op jit(solution)/shard_map/ppermute | solution.py:42
  12.4 0.1 copy.25.refs_2_
  12.5 0.1 copy.26.refs_3_
  12.7 11.4 %shard_map.86 = (f32[4,128,512]{2,1,0:T(8,128)S(1)}, bf16[4,4,512,512]{3,2,1,0:T(8,128)(2,1)S(1)}) custom-call(s32[2]{0:T(128)S(1)} %pad_add_fusion.ranks_ref, f32[2048,4096]{1,0:T(8,128)} %fisher_ref.3, bf16[128,512]{1,0:T(8,128)(2,1)S(1)} %copy.23.refs_0_, bf16[128,512]{1,0:T(8,128)(2,1)S(1)} %copy.24.refs_1_, bf16[128,512]{1,0:T(8,128)(2,1)S(1)} %copy.25.refs_2_, ...), custom_call_target="tpu_custom_call" | custom-call | flops 1073741824 | bytes 16777216 | tf_op jit(solution)/shard_map/pallas_call | solution.py:151
  24.1 3.3 %copy-done.1 = bf16[4,4,512,512]{3,2,1,0:T(8,128)(2,1)} copy-done((bf16[4,4,512,512]{3,2,1,0:T(8,128)(2,1)}, bf16[4,4,512,512]{3,2,1,0:T(8,128)(2,1)S(1)}, u32[]{:S(2)}) %copy-start.1) | copy-done | bytes 8388632
  27.5 5.2 %copy-done = bf16[1024,7168]{1,0:T(8,128)(2,1)S(1)} copy-done((bf16[1024,7168]{1,0:T(8,128)(2,1)S(1)}, bf16[1024,7168]{1,0:T(8,128)(2,1)}, u32[]{:S(2)}) %copy-start) | copy-done | bytes 14680088
  32.6 6.9 %shard_map.89 = (f32[256,256]{1,0:T(8,128)S(1)}, f32[256,256]{1,0:T(8,128)S(1)}, f32[256,256]{1,0:T(8,128)S(1)}, f32[256,256]{1,0:T(8,128)S(1)}) custom-call(s32[2]{0:T(128)S(1)} %pad_add_fusion.ranks_ref, bf16[1024,7168]{1,0:T(8,128)(2,1)S(1)} %copy-done, bf16[1024,2048]{1,0:T(8,128)(2,1)S(1)} %copy-done.5, bf16[7168,128]{1,0:T(8,128)(2,1)S(1)} %copy-done.6, ...), custom_call_target="tpu_custom_call" | custom-call | flops 2415919104 | bytes 18874368 | tf_op jit(solution)/shard_map/pallas_call | solution.py:78
  39.5 1.3 collective-permute-start.10
  40.8 1.5 collective-permute-start.8
  42.3 0.7 collective-permute-start.9
  43.0 0.7 collective-permute-start.15
  43.7 9.7 %collective-permute-start.16 = (bf16[128,512]{0,1:T(8,128)(2,1)S(1)}, bf16[128,512]{0,1:T(8,128)(2,1)S(1)}, u32[]{:S(2)}, u32[]{:S(2)}) collective-permute-start(bf16[128,512]{0,1:T(8,128)(2,1)S(1)} %collective-permute-done.15), channel_id=1, source_target_pairs={{0,2},{1,3},{2,0},{3,1},{4,6},{5,7},{6,4},{7,5},{8,10},{9,11},{10,... | collective-permute-start | bytes 393224 | tf_op jit(solution)/shard_map/ppermute | solution.py:42
  53.4 4.0 %collective-permute-start.17 = (bf16[128,512]{0,1:T(8,128)(2,1)S(1)}, bf16[128,512]{0,1:T(8,128)(2,1)S(1)}, u32[]{:S(2)}, u32[]{:S(2)}) collective-permute-start(bf16[128,512]{0,1:T(8,128)(2,1)S(1)} %collective-permute-done.15), channel_id=1, source_target_pairs={{0,4},{1,5},{2,6},{3,7},{4,0},{5,1},{6,2},{7,3},{8,12},{9,13},{10,... | collective-permute-start | bytes 393224 | tf_op jit(solution)/shard_map/ppermute | solution.py:42
  57.4 0.9 collective-permute-start.18
  58.3 0.4 shard_map.90
  58.8 10.5 %all_to_all.5 = bf16[4,4,32,128]{3,1,2,0:T(4,128)(2,1)S(1)} all-to-all(bf16[4,4,32,128]{3,1,2,0:T(4,128)(2,1)S(1)} %bitcast.44), channel_id=1, replica_groups=mesh['width'=4,'seq'=8] {'width'}, dimensions={0} | all-to-all | bytes 262144 | tf_op jit(solution)/shard_map/all_to_all | solution.py:352
  69.4 1.0 collective-permute-start.11
  70.4 3.4 %collective-permute-start.12 = (bf16[32,16,128]{2,1,0:T(8,128)(2,1)S(1)}, bf16[32,16,128]{2,1,0:T(8,128)(2,1)S(1)}, u32[]{:S(2)}, u32[]{:S(2)}) collective-permute-start(bf16[32,16,128]{2,1,0:T(8,128)(2,1)S(1)} %bitcast.32), channel_id=1, source_target_pairs={{0,4},{1,5},{2,6},{3,7},{4,0},{5,1},{6,2},{7,3},{8,12},{9,13},{10,... | collective-permute-start | bytes 393224 | tf_op jit(solution)/shard_map/ppermute | solution.py:42
  73.9 0.9 pad_maximum_fusion.1
  74.8 0.2 collective-permute-done.11.refs_1_
  75.0 6.4 %collective-permute-done.12.refs_2_ = bf16[32,16,128]{2,1,0:T(8,128)(2,1)S(1)} collective-permute-done((bf16[32,16,128]{2,1,0:T(8,128)(2,1)S(1)}, bf16[32,16,128]{2,1,0:T(8,128)(2,1)S(1)}, u32[]{:S(2)}, u32[]{:S(2)}) %collective-permute-start.12) | collective-permute-done | bytes 131104 | tf_op jit(solution)/shard_map/ppermute | solution.py:42
  81.4 0.9 pad_maximum_fusion
  82.3 11.1 %shard_map.85 = (f32[4,128,512]{2,1,0:T(8,128)S(1)}, bf16[4,4,512,512]{3,2,1,0:T(8,128)(2,1)S(1)}) custom-call(s32[2]{0:T(128)S(1)} %pad_add_fusion.ranks_ref, f32[2048,4096]{1,0:T(8,128)} %fisher_ref.3, bf16[128,512]{1,0:T(8,128)(2,1)S(1)} %copy.23.refs_0_, bf16[128,512]{1,0:T(8,128)(2,1)S(1)} %copy.24.refs_1_, bf16[128,512]{1,0:T(8,128)(2,1)S(1)} %copy.25.refs_2_, ...), custom_call_target="tpu_custom_call" | custom-call | flops 1073741824 | bytes 16777216 | tf_op jit(solution)/shard_map/pallas_call | solution.py:151
  93.3 3.2 %copy-done.3 = bf16[4,4,512,512]{3,2,1,0:T(8,128)(2,1)} copy-done((bf16[4,4,512,512]{3,2,1,0:T(8,128)(2,1)}, bf16[4,4,512,512]{3,2,1,0:T(8,128)(2,1)S(1)}, u32[]{:S(2)}) %copy-start.3) | copy-done | bytes 8388632
  96.7 1.9 %collective-permute-start.4 = (bf16[128,512]{1,0:T(8,128)(2,1)S(1)}, bf16[128,512]{1,0:T(8,128)(2,1)S(1)}, u32[]{:S(2)}, u32[]{:S(2)}) collective-permute-start(bf16[128,512]{1,0:T(8,128)(2,1)S(1)} %get-tuple-element.30), channel_id=1, source_target_pairs={{0,2},{1,3},{2,0},{3,1},{4,6},{5,7},{6,4},{7,5},{8,10},{9,11},{10,... | collective-permute-start | bytes 393224 | tf_op jit(solution)/shard_map/ppermute | solution.py:42
  98.6 1.2 collective-permute-start.5
  99.8 1.4 collective-permute-start.6
  101.2 3.9 %collective-permute-done.4.refs_1_ = bf16[128,512]{1,0:T(8,128)(2,1)S(1)} collective-permute-done((bf16[128,512]{1,0:T(8,128)(2,1)S(1)}, bf16[128,512]{1,0:T(8,128)(2,1)S(1)}, u32[]{:S(2)}, u32[]{:S(2)}) %collective-permute-start.4) | collective-permute-done | bytes 131104 | tf_op jit(solution)/shard_map/ppermute | solution.py:42
  105.1 6.4 %collective-permute-done.5.refs_2_ = bf16[128,512]{1,0:T(8,128)(2,1)S(1)} collective-permute-done((bf16[128,512]{1,0:T(8,128)(2,1)S(1)}, bf16[128,512]{1,0:T(8,128)(2,1)S(1)}, u32[]{:S(2)}, u32[]{:S(2)}) %collective-permute-start.5) | collective-permute-done | bytes 131104 | tf_op jit(solution)/shard_map/ppermute | solution.py:42
  111.6 2.7 %collective-permute-start.24 = (bf16[128,512]{1,0:T(8,128)(2,1)S(1)}, bf16[128,512]{1,0:T(8,128)(2,1)S(1)}, u32[]{:S(2)}, u32[]{:S(2)}) collective-permute-start(bf16[128,512]{1,0:T(8,128)(2,1)S(1)} %shard_map.88.refs_0_), channel_id=1, source_target_pairs={{0,2},{1,3},{2,0},{3,1},{4,6},{5,7},{6,4},{7,5},{8,10},{9,11},{10,... | collective-permute-start | bytes 393224 | tf_op jit(solution)/shard_map/ppermute | solution.py:42
  114.3 1.2 collective-permute-start.25
  115.5 1.4 collective-permute-start.26
  116.9 1.9 %collective-permute-done.24.refs_1_ = bf16[128,512]{1,0:T(8,128)(2,1)S(1)} collective-permute-done((bf16[128,512]{1,0:T(8,128)(2,1)S(1)}, bf16[128,512]{1,0:T(8,128)(2,1)S(1)}, u32[]{:S(2)}, u32[]{:S(2)}) %collective-permute-start.24) | collective-permute-done | bytes 131104 | tf_op jit(solution)/shard_map/ppermute | solution.py:42
  118.7 8.0 %collective-permute-done.25.refs_2_ = bf16[128,512]{1,0:T(8,128)(2,1)S(1)} collective-permute-done((bf16[128,512]{1,0:T(8,128)(2,1)S(1)}, bf16[128,512]{1,0:T(8,128)(2,1)S(1)}, u32[]{:S(2)}, u32[]{:S(2)}) %collective-permute-start.25) | collective-permute-done | bytes 131104 | tf_op jit(solution)/shard_map/ppermute | solution.py:42
  126.8 0.9 pad_maximum_fusion.2
  127.7 0.1 copy.33.refs_5_
  127.8 0.1 copy.34.refs_6_
  127.9 0.1 copy.35.refs_7_
  128.0 0.1 copy.36.refs_8_
  128.2 1.2 copy.37.refs_9_
  129.4 1.0 shard_map.91
  130.4 1.6 collective-permute-start.21
  132.0 0.7 collective-permute-start.22
  132.7 1.4 collective-permute-start.23
  134.1 0.7 collective-permute-start.20
  134.8 0.2 collective-permute-done.21
  135.0 1.3 collective-permute-done.22
  136.2 1.7 %collective-permute-done.23 = f32[128,128]{1,0:T(8,128)S(1)} collective-permute-done((f32[128,128]{1,0:T(8,128)S(1)}, f32[128,128]{1,0:T(8,128)S(1)}, u32[]{:S(2)}, u32[]{:S(2)}) %collective-permute-start.23) | collective-permute-done | bytes 65568 | tf_op jit(solution)/shard_map/ppermute | solution.py:42
  138.0 0.7 collective-permute-start.7
  138.7 3.4 %copy-done.2 = bf16[4,4,512,512]{3,2,1,0:T(8,128)(2,1)S(1)} copy-done((bf16[4,4,512,512]{3,2,1,0:T(8,128)(2,1)S(1)}, bf16[4,4,512,512]{3,2,1,0:T(8,128)(2,1)}, u32[]{:S(2)}) %copy-start.2) | copy-done | bytes 8388632
  142.1 3.4 %copy-done.4 = bf16[4,4,512,512]{3,2,1,0:T(8,128)(2,1)S(1)} copy-done((bf16[4,4,512,512]{3,2,1,0:T(8,128)(2,1)S(1)}, bf16[4,4,512,512]{3,2,1,0:T(8,128)(2,1)}, u32[]{:S(2)}) %copy-start.4) | copy-done | bytes 8388632
  145.5 6.0 %shard_map.92 = (f32[4,512,256]{2,1,0:T(8,128)S(1)}, f32[128,256]{1,0:T(8,128)S(1)}) custom-call(bf16[4,4,512,512]{3,2,1,0:T(8,128)(2,1)S(1)} %copy-done.4, bf16[4,4,512,512]{3,2,1,0:T(8,128)(2,1)S(1)} %copy-done.2, bf16[128,512]{1,0:T(8,128)(2,1)S(1)} %shard_map.88.refs_0_, bf16[128,512]{1,0:T(8,128)(2,1)S(1)} %collective-permute-done.24.refs_1_, ...), custom_call_target="tpu_custom_call" | custom-call | flops 4294967296 | bytes 18874368 | tf_op jit(solution)/shard_map/pallas_call | solution.py:47
  151.4 1.1 shard_map.93
  152.5 5.4 %collective-permute-start.31 = (bf16[512,128]{1,0:T(8,128)(2,1)S(1)}, bf16[512,128]{1,0:T(8,128)(2,1)S(1)}, u32[]{:S(2)}, u32[]{:S(2)}) collective-permute-start(bf16[512,128]{1,0:T(8,128)(2,1)S(1)} %get-tuple-element.45), channel_id=1, source_target_pairs={{0,8},{8,0},{16,24},{24,16},{1,9},{9,1},{17,25},{25,17},{2,10},{10... | collective-permute-start | bytes 393224 | tf_op jit(solution)/shard_map/ppermute | solution.py:42
  157.9 3.7 %collective-permute-start.32 = (bf16[512,128]{1,0:T(8,128)(2,1)S(1)}, bf16[512,128]{1,0:T(8,128)(2,1)S(1)}, u32[]{:S(2)}, u32[]{:S(2)}) collective-permute-start(bf16[512,128]{1,0:T(8,128)(2,1)S(1)} %get-tuple-element.46), channel_id=1, source_target_pairs={{0,16},{8,24},{16,0},{24,8},{1,17},{9,25},{17,1},{25,9},{2,18},{10... | collective-permute-start | bytes 393224 | tf_op jit(solution)/shard_map/ppermute | solution.py:42
  161.6 1.8 %collective-permute-start.29 = (f32[128,128]{1,0:T(8,128)S(1)}, f32[128,128]{1,0:T(8,128)S(1)}, u32[]{:S(2)}, u32[]{:S(2)}) collective-permute-start(f32[128,128]{1,0:T(8,128)S(1)} %get-tuple-element.43.refs_0_), channel_id=1, source_target_pairs={{0,16},{8,24},{16,0},{24,8},{1,17},{9,25},{17,1},{25,9},{2,18},{10... | collective-permute-start | bytes 196616 | tf_op jit(solution)/shard_map/ppermute | solution.py:42
  163.4 3.4 %collective-permute-start.30 = (f32[128,128]{1,0:T(8,128)S(1)}, f32[128,128]{1,0:T(8,128)S(1)}, u32[]{:S(2)}, u32[]{:S(2)}) collective-permute-start(f32[128,128]{1,0:T(8,128)S(1)} %get-tuple-element.43.refs_0_), channel_id=1, source_target_pairs={{0,24},{8,16},{16,8},{24,0},{1,25},{9,17},{17,9},{25,1},{2,26},{10... | collective-permute-start | bytes 196616 | tf_op jit(solution)/shard_map/ppermute | solution.py:42
  166.9 4.6 %collective-permute-done.29.refs_2_ = f32[128,128]{1,0:T(8,128)S(1)} collective-permute-done((f32[128,128]{1,0:T(8,128)S(1)}, f32[128,128]{1,0:T(8,128)S(1)}, u32[]{:S(2)}, u32[]{:S(2)}) %collective-permute-start.29) | collective-permute-done | bytes 65568 | tf_op jit(solution)/shard_map/ppermute | solution.py:42
  171.5 2.0 %shard_map.94 = (f32[512,128]{1,0:T(8,128)}, f32[512,128]{1,0:T(8,128)}, f32[4,128]{1,0:T(4,128)}) custom-call(s32[2]{0:T(128)S(1)} %pad_add_fusion.ranks_ref, f32[512,128]{1,0:T(8,128)S(1)} %bitcast.36, bf16[128,512]{1,0:T(8,128)(2,1)S(1)} %collective-permute-done.7.y_ref, bf16[128,512]{1,0:T(8,128)(2,1)S(1)} %collective-permute-done.20.g_ref, ...), custom_call_target="tpu_custom_call" | custom-call | bytes 1507336 | tf_op jit(solution)/shard_map/pallas_call | solution.py:47
  (51 shorter events, 0.7 us)
Async XLA Ops:
  1.6 6.9 %collective-permute-start = (bf16[128,512]{0,1:T(8,128)(2,1)S(1)}, bf16[128,512]{0,1:T(8,128)(2,1)S(1)}, u32[]{:S(2)}, u32[]{:S(2)}) collective-permute-start(bf16[128,512]{0,1:T(8,128)(2,1)S(1)} %convert_bitcast_fusion), channel_id=1, source_target_pairs={{0,8},{8,0},{16,24},{24,16},{1,9},{9,1},{17,25},{25,17},{2,10},{10... | collective-permute-start | bytes 393224 | tf_op jit(solution)/shard_map/ppermute | solution.py:42
  4.6 7.8 %collective-permute-start.1 = (bf16[128,512]{0,1:T(8,128)(2,1)S(1)}, bf16[128,512]{0,1:T(8,128)(2,1)S(1)}, u32[]{:S(2)}, u32[]{:S(2)}) collective-permute-start(bf16[128,512]{0,1:T(8,128)(2,1)S(1)} %convert_bitcast_fusion), channel_id=1, source_target_pairs={{0,16},{8,24},{16,0},{24,8},{1,17},{9,25},{17,1},{25,9},{2,18},{10... | collective-permute-start | bytes 393224 | tf_op jit(solution)/shard_map/ppermute | solution.py:42
  6.1 6.4 %collective-permute-start.2 = (bf16[128,512]{0,1:T(8,128)(2,1)S(1)}, bf16[128,512]{0,1:T(8,128)(2,1)S(1)}, u32[]{:S(2)}, u32[]{:S(2)}) collective-permute-start(bf16[128,512]{0,1:T(8,128)(2,1)S(1)} %convert_bitcast_fusion), channel_id=1, source_target_pairs={{0,24},{8,16},{16,8},{24,0},{1,25},{9,17},{17,9},{25,1},{2,26},{10... | collective-permute-start | bytes 393224 | tf_op jit(solution)/shard_map/ppermute | solution.py:42
  12.6 14.8 %copy-start.5 = (bf16[1024,2048]{1,0:T(8,128)(2,1)S(1)}, bf16[1024,2048]{1,0:T(8,128)(2,1)}, u32[]{:S(2)}) copy-start(bf16[1024,2048]{1,0:T(8,128)(2,1)} %err_ref.1) | copy-start | bytes 12582916
  12.6 14.8 %copy-start.6 = (bf16[7168,128]{1,0:T(8,128)(2,1)S(1)}, bf16[7168,128]{1,0:T(8,128)(2,1)}, u32[]{:S(2)}) copy-start(bf16[7168,128]{1,0:T(8,128)(2,1)} %pa_ref.1) | copy-start | bytes 5505028
  12.7 14.8 %copy-start.8 = (bf16[2048,128]{1,0:T(8,128)(2,1)S(1)}, bf16[2048,128]{1,0:T(8,128)(2,1)}, u32[]{:S(2)}) copy-start(bf16[2048,128]{1,0:T(8,128)(2,1)} %pe_ref.1) | copy-start | bytes 1572868
  24.1 3.3 %copy-start.1 = (bf16[4,4,512,512]{3,2,1,0:T(8,128)(2,1)}, bf16[4,4,512,512]{3,2,1,0:T(8,128)(2,1)S(1)}, u32[]{:S(2)}) copy-start(bf16[4,4,512,512]{3,2,1,0:T(8,128)(2,1)S(1)} %get-tuple-element.40.odd_ref) | copy-start | bytes 25165828
  27.4 69.2 %collective-permute-start.3 = (f32[4,128,512]{2,1,0:T(8,128)S(1)}, f32[4,128,512]{2,1,0:T(8,128)S(1)}, u32[]{:S(2)}, u32[]{:S(2)}) collective-permute-start(f32[4,128,512]{2,1,0:T(8,128)S(1)} %get-tuple-element.28), channel_id=1, source_target_pairs={{0,1},{1,0},{2,3},{3,2},{4,5},{5,4},{6,7},{7,6},{8,9},{9,8},{10,11... | collective-permute-start | bytes 3145736 | tf_op jit(solution)/shard_map/ppermute | solution.py:42
  27.4 5.2 %copy-start = (bf16[1024,7168]{1,0:T(8,128)(2,1)S(1)}, bf16[1024,7168]{1,0:T(8,128)(2,1)}, u32[]{:S(2)}) copy-start(bf16[1024,7168]{1,0:T(8,128)(2,1)} %act_ref.1) | copy-start | bytes 44040196
  39.5 13.9 %collective-permute-start.10 = (f32[256,256]{1,0:T(8,128)S(1)}, f32[256,256]{1,0:T(8,128)S(1)}, u32[]{:S(2)}, u32[]{:S(2)}) collective-permute-start(f32[256,256]{1,0:T(8,128)S(1)} %get-tuple-element.36), channel_id=1, source_target_pairs={{0,24},{8,16},{16,8},{24,0},{1,25},{9,17},{17,9},{25,1},{2,26},{10... | collective-permute-start | bytes 786440 | tf_op jit(solution)/shard_map/ppermute | solution.py:42
  40.8 16.6 %collective-permute-start.8 = (f32[256,256]{1,0:T(8,128)S(1)}, f32[256,256]{1,0:T(8,128)S(1)}, u32[]{:S(2)}, u32[]{:S(2)}) collective-permute-start(f32[256,256]{1,0:T(8,128)S(1)} %get-tuple-element.34), channel_id=1, source_target_pairs={{0,8},{8,0},{16,24},{24,16},{1,9},{9,1},{17,25},{25,17},{2,10},{10... | collective-permute-start | bytes 786440 | tf_op jit(solution)/shard_map/ppermute | solution.py:42
  42.3 15.9 %collective-permute-start.9 = (f32[256,256]{1,0:T(8,128)S(1)}, f32[256,256]{1,0:T(8,128)S(1)}, u32[]{:S(2)}, u32[]{:S(2)}) collective-permute-start(f32[256,256]{1,0:T(8,128)S(1)} %get-tuple-element.35), channel_id=1, source_target_pairs={{0,16},{8,24},{16,0},{24,8},{1,17},{9,25},{17,1},{25,9},{2,18},{10... | collective-permute-start | bytes 786440 | tf_op jit(solution)/shard_map/ppermute | solution.py:42
  43.0 0.7 collective-permute-start.15
  43.7 26.7 %collective-permute-start.16 = (bf16[128,512]{0,1:T(8,128)(2,1)S(1)}, bf16[128,512]{0,1:T(8,128)(2,1)S(1)}, u32[]{:S(2)}, u32[]{:S(2)}) collective-permute-start(bf16[128,512]{0,1:T(8,128)(2,1)S(1)} %collective-permute-done.15), channel_id=1, source_target_pairs={{0,2},{1,3},{2,0},{3,1},{4,6},{5,7},{6,4},{7,5},{8,10},{9,11},{10,... | collective-permute-start | bytes 393224 | tf_op jit(solution)/shard_map/ppermute | solution.py:42
  53.4 20.5 %collective-permute-start.17 = (bf16[128,512]{0,1:T(8,128)(2,1)S(1)}, bf16[128,512]{0,1:T(8,128)(2,1)S(1)}, u32[]{:S(2)}, u32[]{:S(2)}) collective-permute-start(bf16[128,512]{0,1:T(8,128)(2,1)S(1)} %collective-permute-done.15), channel_id=1, source_target_pairs={{0,4},{1,5},{2,6},{3,7},{4,0},{5,1},{6,2},{7,3},{8,12},{9,13},{10,... | collective-permute-start | bytes 393224 | tf_op jit(solution)/shard_map/ppermute | solution.py:42
  57.4 16.4 %collective-permute-start.18 = (bf16[128,512]{0,1:T(8,128)(2,1)S(1)}, bf16[128,512]{0,1:T(8,128)(2,1)S(1)}, u32[]{:S(2)}, u32[]{:S(2)}) collective-permute-start(bf16[128,512]{0,1:T(8,128)(2,1)S(1)} %collective-permute-done.15), channel_id=1, source_target_pairs={{0,6},{1,7},{2,4},{3,5},{4,2},{5,3},{6,0},{7,1},{8,14},{9,15},{10,... | collective-permute-start | bytes 393224 | tf_op jit(solution)/shard_map/ppermute | solution.py:42
  69.4 5.6 %collective-permute-start.11 = (bf16[32,16,128]{2,1,0:T(8,128)(2,1)S(1)}, bf16[32,16,128]{2,1,0:T(8,128)(2,1)S(1)}, u32[]{:S(2)}, u32[]{:S(2)}) collective-permute-start(bf16[32,16,128]{2,1,0:T(8,128)(2,1)S(1)} %bitcast.31), channel_id=1, source_target_pairs={{0,2},{1,3},{2,0},{3,1},{4,6},{5,7},{6,4},{7,5},{8,10},{9,11},{10,... | collective-permute-start | bytes 393224 | tf_op jit(solution)/shard_map/ppermute | solution.py:42
  70.4 11.0 %collective-permute-start.12 = (bf16[32,16,128]{2,1,0:T(8,128)(2,1)S(1)}, bf16[32,16,128]{2,1,0:T(8,128)(2,1)S(1)}, u32[]{:S(2)}, u32[]{:S(2)}) collective-permute-start(bf16[32,16,128]{2,1,0:T(8,128)(2,1)S(1)} %bitcast.32), channel_id=1, source_target_pairs={{0,4},{1,5},{2,6},{3,7},{4,0},{5,1},{6,2},{7,3},{8,12},{9,13},{10,... | collective-permute-start | bytes 393224 | tf_op jit(solution)/shard_map/ppermute | solution.py:42
  73.8 7.5 %collective-permute-start.13 = (bf16[32,16,128]{2,1,0:T(8,128)(2,1)S(1)}, bf16[32,16,128]{2,1,0:T(8,128)(2,1)S(1)}, u32[]{:S(2)}, u32[]{:S(2)}) collective-permute-start(bf16[32,16,128]{2,1,0:T(8,128)(2,1)S(1)} %bitcast.33), channel_id=1, source_target_pairs={{0,6},{1,7},{2,4},{3,5},{4,2},{5,3},{6,0},{7,1},{8,14},{9,15},{10,... | collective-permute-start | bytes 393224 | tf_op jit(solution)/shard_map/ppermute | solution.py:42
  74.7 53.4 %collective-permute-start.19 = (bf16[4,128,512]{1,2,0:T(8,128)(2,1)}, bf16[4,128,512]{1,2,0:T(8,128)(2,1)}, u32[]{:S(2)}, u32[]{:S(2)}) collective-permute-start(bf16[4,128,512]{1,2,0:T(8,128)(2,1)} %pad_maximum_fusion.1), channel_id=1, source_target_pairs={{0,1},{1,0},{2,3},{3,2},{4,5},{5,4},{6,7},{7,6},{8,9},{9,8},{10,11... | collective-permute-start | bytes 1572872 | tf_op jit(solution)/shard_map/ppermute | solution.py:42
  82.3 47.1 %collective-permute-start.14 = (bf16[4,32,16,128]{3,2,1,0:T(8,128)(2,1)}, bf16[4,32,16,128]{3,2,1,0:T(8,128)(2,1)S(1)}, u32[]{:S(2)}, u32[]{:S(2)}) collective-permute-start(bf16[4,32,16,128]{3,2,1,0:T(8,128)(2,1)} %pad_maximum_fusion), channel_id=1, source_target_pairs={{0,1},{1,0},{2,3},{3,2},{4,5},{5,4},{6,7},{7,6},{8,9},{9,8},{10,11... | collective-permute-start | bytes 1572872 | tf_op jit(solution)/shard_map/ppermute | solution.py:42
  93.3 3.2 %copy-start.3 = (bf16[4,4,512,512]{3,2,1,0:T(8,128)(2,1)}, bf16[4,4,512,512]{3,2,1,0:T(8,128)(2,1)S(1)}, u32[]{:S(2)}) copy-start(bf16[4,4,512,512]{3,2,1,0:T(8,128)(2,1)S(1)} %get-tuple-element.39.even_ref) | copy-start | bytes 25165828
  96.7 8.4 %collective-permute-start.4 = (bf16[128,512]{1,0:T(8,128)(2,1)S(1)}, bf16[128,512]{1,0:T(8,128)(2,1)S(1)}, u32[]{:S(2)}, u32[]{:S(2)}) collective-permute-start(bf16[128,512]{1,0:T(8,128)(2,1)S(1)} %get-tuple-element.30), channel_id=1, source_target_pairs={{0,2},{1,3},{2,0},{3,1},{4,6},{5,7},{6,4},{7,5},{8,10},{9,11},{10,... | collective-permute-start | bytes 393224 | tf_op jit(solution)/shard_map/ppermute | solution.py:42
  98.6 12.9 %collective-permute-start.5 = (bf16[128,512]{1,0:T(8,128)(2,1)S(1)}, bf16[128,512]{1,0:T(8,128)(2,1)S(1)}, u32[]{:S(2)}, u32[]{:S(2)}) collective-permute-start(bf16[128,512]{1,0:T(8,128)(2,1)S(1)} %get-tuple-element.31), channel_id=1, source_target_pairs={{0,4},{1,5},{2,6},{3,7},{4,0},{5,1},{6,2},{7,3},{8,12},{9,13},{10,... | collective-permute-start | bytes 393224 | tf_op jit(solution)/shard_map/ppermute | solution.py:42
  99.8 11.7 %collective-permute-start.6 = (bf16[128,512]{1,0:T(8,128)(2,1)S(1)}, bf16[128,512]{1,0:T(8,128)(2,1)S(1)}, u32[]{:S(2)}, u32[]{:S(2)}) collective-permute-start(bf16[128,512]{1,0:T(8,128)(2,1)S(1)} %get-tuple-element.32), channel_id=1, source_target_pairs={{0,6},{1,7},{2,4},{3,5},{4,2},{5,3},{6,0},{7,1},{8,14},{9,15},{10,... | collective-permute-start | bytes 393224 | tf_op jit(solution)/shard_map/ppermute | solution.py:42
  111.6 7.2 %collective-permute-start.24 = (bf16[128,512]{1,0:T(8,128)(2,1)S(1)}, bf16[128,512]{1,0:T(8,128)(2,1)S(1)}, u32[]{:S(2)}, u32[]{:S(2)}) collective-permute-start(bf16[128,512]{1,0:T(8,128)(2,1)S(1)} %shard_map.88.refs_0_), channel_id=1, source_target_pairs={{0,2},{1,3},{2,0},{3,1},{4,6},{5,7},{6,4},{7,5},{8,10},{9,11},{10,... | collective-permute-start | bytes 393224 | tf_op jit(solution)/shard_map/ppermute | solution.py:42
  114.3 12.5 %collective-permute-start.25 = (bf16[128,512]{1,0:T(8,128)(2,1)S(1)}, bf16[128,512]{1,0:T(8,128)(2,1)S(1)}, u32[]{:S(2)}, u32[]{:S(2)}) collective-permute-start(bf16[128,512]{1,0:T(8,128)(2,1)S(1)} %shard_map.88.refs_0_), channel_id=1, source_target_pairs={{0,4},{1,5},{2,6},{3,7},{4,0},{5,1},{6,2},{7,3},{8,12},{9,13},{10,... | collective-permute-start | bytes 393224 | tf_op jit(solution)/shard_map/ppermute | solution.py:42
  115.5 11.3 %collective-permute-start.26 = (bf16[128,512]{1,0:T(8,128)(2,1)S(1)}, bf16[128,512]{1,0:T(8,128)(2,1)S(1)}, u32[]{:S(2)}, u32[]{:S(2)}) collective-permute-start(bf16[128,512]{1,0:T(8,128)(2,1)S(1)} %shard_map.88.refs_0_), channel_id=1, source_target_pairs={{0,6},{1,7},{2,4},{3,5},{4,2},{5,3},{6,0},{7,1},{8,14},{9,15},{10,... | collective-permute-start | bytes 393224 | tf_op jit(solution)/shard_map/ppermute | solution.py:42
  127.7 11.0 %collective-permute-start.27 = (bf16[4,128,512]{2,1,0:T(8,128)(2,1)}, bf16[4,128,512]{2,1,0:T(8,128)(2,1)S(1)}, u32[]{:S(2)}, u32[]{:S(2)}) collective-permute-start(bf16[4,128,512]{2,1,0:T(8,128)(2,1)} %pad_maximum_fusion.2), channel_id=1, source_target_pairs={{0,1},{1,0},{2,3},{3,2},{4,5},{5,4},{6,7},{7,6},{8,9},{9,8},{10,11... | collective-permute-start | bytes 1572872 | tf_op jit(solution)/shard_map/ppermute | solution.py:42
  130.4 4.6 %collective-permute-start.21 = (f32[128,128]{1,0:T(8,128)S(1)}, f32[128,128]{1,0:T(8,128)S(1)}, u32[]{:S(2)}, u32[]{:S(2)}) collective-permute-start(f32[128,128]{1,0:T(8,128)S(1)} %get-tuple-element.38), channel_id=1, source_target_pairs={{0,8},{8,0},{16,24},{24,16},{1,9},{9,1},{17,25},{25,17},{2,10},{10... | collective-permute-start | bytes 196616 | tf_op jit(solution)/shard_map/ppermute | solution.py:42
  132.0 4.3 %collective-permute-start.22 = (f32[128,128]{1,0:T(8,128)S(1)}, f32[128,128]{1,0:T(8,128)S(1)}, u32[]{:S(2)}, u32[]{:S(2)}) collective-permute-start(f32[128,128]{1,0:T(8,128)S(1)} %get-tuple-element.38), channel_id=1, source_target_pairs={{0,16},{8,24},{16,0},{24,8},{1,17},{9,25},{17,1},{25,9},{2,18},{10... | collective-permute-start | bytes 196616 | tf_op jit(solution)/shard_map/ppermute | solution.py:42
  132.7 5.3 %collective-permute-start.23 = (f32[128,128]{1,0:T(8,128)S(1)}, f32[128,128]{1,0:T(8,128)S(1)}, u32[]{:S(2)}, u32[]{:S(2)}) collective-permute-start(f32[128,128]{1,0:T(8,128)S(1)} %get-tuple-element.38), channel_id=1, source_target_pairs={{0,24},{8,16},{16,8},{24,0},{1,25},{9,17},{17,9},{25,1},{2,26},{10... | collective-permute-start | bytes 196616 | tf_op jit(solution)/shard_map/ppermute | solution.py:42
  134.1 27.5 %collective-permute-start.20 = (bf16[128,512]{1,0:T(8,128)(2,1)S(1)}, bf16[128,512]{1,0:T(8,128)(2,1)S(1)}, u32[]{:S(2)}, u32[]{:S(2)}) collective-permute-start(bf16[128,512]{1,0:T(8,128)(2,1)S(1)} %slice_bitcast_fusion), channel_id=1, source_target_pairs={{0,0},{1,8},{2,16},{3,24},{4,1},{5,9},{6,17},{7,25},{8,2},{9,10},{... | collective-permute-start | bytes 393224 | tf_op jit(solution)/shard_map/ppermute | solution.py:358
  138.0 23.6 %collective-permute-start.7 = (bf16[128,512]{1,0:T(8,128)(2,1)S(1)}, bf16[128,512]{1,0:T(8,128)(2,1)S(1)}, u32[]{:S(2)}, u32[]{:S(2)}) collective-permute-start(bf16[128,512]{1,0:T(8,128)(2,1)S(1)} %shard_map.88.refs_0_), channel_id=1, source_target_pairs={{0,0},{1,8},{2,16},{3,24},{4,1},{5,9},{6,17},{7,25},{8,2},{9,10},{... | collective-permute-start | bytes 393224 | tf_op jit(solution)/shard_map/ppermute | solution.py:366
  138.7 3.4 %copy-start.2 = (bf16[4,4,512,512]{3,2,1,0:T(8,128)(2,1)S(1)}, bf16[4,4,512,512]{3,2,1,0:T(8,128)(2,1)}, u32[]{:S(2)}) copy-start(bf16[4,4,512,512]{3,2,1,0:T(8,128)(2,1)} %copy-done.1) | copy-start | bytes 25165828
  142.1 3.4 %copy-start.4 = (bf16[4,4,512,512]{3,2,1,0:T(8,128)(2,1)S(1)}, bf16[4,4,512,512]{3,2,1,0:T(8,128)(2,1)}, u32[]{:S(2)}) copy-start(bf16[4,4,512,512]{3,2,1,0:T(8,128)(2,1)} %copy-done.3) | copy-start | bytes 25165828
  145.5 26.0 %copy-start.7 = (f32[1,512,128]{2,1,0:T(8,128)S(1)}, f32[1,512,128]{2,1,0:T(8,128)}, u32[]{:S(2)}) copy-start(f32[1,512,128]{2,1,0:T(8,128)} %param.11) | copy-start | bytes 786436
  152.5 19.0 %collective-permute-start.31 = (bf16[512,128]{1,0:T(8,128)(2,1)S(1)}, bf16[512,128]{1,0:T(8,128)(2,1)S(1)}, u32[]{:S(2)}, u32[]{:S(2)}) collective-permute-start(bf16[512,128]{1,0:T(8,128)(2,1)S(1)} %get-tuple-element.45), channel_id=1, source_target_pairs={{0,8},{8,0},{16,24},{24,16},{1,9},{9,1},{17,25},{25,17},{2,10},{10... | collective-permute-start | bytes 393224 | tf_op jit(solution)/shard_map/ppermute | solution.py:42
  157.8 5.6 %collective-permute-start.28 = (f32[128,128]{1,0:T(8,128)S(1)}, f32[128,128]{1,0:T(8,128)S(1)}, u32[]{:S(2)}, u32[]{:S(2)}) collective-permute-start(f32[128,128]{1,0:T(8,128)S(1)} %get-tuple-element.43.refs_0_), channel_id=1, source_target_pairs={{0,8},{8,0},{16,24},{24,16},{1,9},{9,1},{17,25},{25,17},{2,10},{10... | collective-permute-start | bytes 196616 | tf_op jit(solution)/shard_map/ppermute | solution.py:42
  157.9 13.5 %collective-permute-start.32 = (bf16[512,128]{1,0:T(8,128)(2,1)S(1)}, bf16[512,128]{1,0:T(8,128)(2,1)S(1)}, u32[]{:S(2)}, u32[]{:S(2)}) collective-permute-start(bf16[512,128]{1,0:T(8,128)(2,1)S(1)} %get-tuple-element.46), channel_id=1, source_target_pairs={{0,16},{8,24},{16,0},{24,8},{1,17},{9,25},{17,1},{25,9},{2,18},{10... | collective-permute-start | bytes 393224 | tf_op jit(solution)/shard_map/ppermute | solution.py:42
  161.6 9.8 %collective-permute-start.33 = (bf16[512,128]{1,0:T(8,128)(2,1)S(1)}, bf16[512,128]{1,0:T(8,128)(2,1)S(1)}, u32[]{:S(2)}, u32[]{:S(2)}) collective-permute-start(bf16[512,128]{1,0:T(8,128)(2,1)S(1)} %get-tuple-element.47), channel_id=1, source_target_pairs={{0,24},{8,16},{16,8},{24,0},{1,25},{9,17},{17,9},{25,1},{2,26},{10... | collective-permute-start | bytes 393224 | tf_op jit(solution)/shard_map/ppermute | solution.py:42
  161.6 9.8 %collective-permute-start.29 = (f32[128,128]{1,0:T(8,128)S(1)}, f32[128,128]{1,0:T(8,128)S(1)}, u32[]{:S(2)}, u32[]{:S(2)}) collective-permute-start(f32[128,128]{1,0:T(8,128)S(1)} %get-tuple-element.43.refs_0_), channel_id=1, source_target_pairs={{0,16},{8,24},{16,0},{24,8},{1,17},{9,25},{17,1},{25,9},{2,18},{10... | collective-permute-start | bytes 196616 | tf_op jit(solution)/shard_map/ppermute | solution.py:42
  163.4 8.0 %collective-permute-start.30 = (f32[128,128]{1,0:T(8,128)S(1)}, f32[128,128]{1,0:T(8,128)S(1)}, u32[]{:S(2)}, u32[]{:S(2)}) collective-permute-start(f32[128,128]{1,0:T(8,128)S(1)} %get-tuple-element.43.refs_0_), channel_id=1, source_target_pairs={{0,24},{8,16},{16,8},{24,0},{1,25},{9,17},{17,9},{25,1},{2,26},{10... | collective-permute-start | bytes 196616 | tf_op jit(solution)/shard_map/ppermute | solution.py:42

commit v2 on v0

v2 whole, which is shorter than its diff:
```python
import jax
import jax.numpy as jnp
from jax import lax
from jax.experimental import pallas as pl
from jax.experimental.pallas import tpu as pltpu
from jax.sharding import PartitionSpec as P

SEQ_LEN = 64

ridge_damp = 0.1
bound_low = 0.5
bound_high = 6.0
center = 0.5 * (bound_high + bound_low)
half_width = 0.5 * (bound_high - bound_low)
rho_first = half_width / center
rho_second = 1.0 / (2.0 * center / half_width - rho_first)
fall = rho_second * rho_first
lead = (1.0 + fall) / center
tail = 2.0 * rho_second / half_width / center

BF16 = jnp.bfloat16
F32 = jnp.float32
HIGHEST = lax.Precision.HIGHEST
MIB = 1024 * 1024
NN = (((1,), (0,)), ((), ()))
NT = (((1,), (1,)), ((), ()))
TN = (((0,), (0,)), ((), ()))

WHOLE = pl.BlockSpec(memory_space=pltpu.VMEM)
SCALARS = pl.BlockSpec(memory_space=pltpu.SMEM)


BRIEF = pl.CostEstimate(flops=1, bytes_accessed=1, transcendentals=0)


def shaped(shape, dtype):
    return jax.ShapeDtypeStruct(shape, dtype)


def dot(a, b, dims, precision=None):
    return lax.dot_general(a, b, dims, precision=precision, preferred_element_type=F32)


def swap(x, axis, k):
    return lax.ppermute(x, axis, [(i, i ^ k) for i in range(lax.axis_size(axis))])


def call(body, out, args, flops=0, limit=8, **kw):
    return pl.pallas_call(
        body,
        out_shape=out,
        compiler_params=pltpu.CompilerParams(vmem_limit_bytes=limit * MIB),
        cost_estimate=BRIEF,
        **kw,
    )(*args)


def project(ranks, activations, errors, proj_acts, proj_errs, n_w):
    tokens, feats_a = activations.shape
    feats_e = errors.shape[1]
    rank = proj_acts.shape[1]
    own = tokens // n_w
    rows = min(256, own)
    per = own // rows
    half = feats_a // 2
    order = [(r, h) for r in range(n_w - 1, -1, -1) for _ in range(per) for h in range(2)]
    depth = min(4, len(order))

    def body(ranks_ref, act_ref, err_ref, pa_ref, pe_ref, *refs):
        outs = refs[:n_w]
        pa, pe, act, err, wsems, sems = refs[n_w:]

        def copies(n):
            r, h = order[n]
            at = ((ranks_ref[0] ^ r) * per + n // 2 % per) * rows
            some = pl.ds(pl.multiple_of(at, rows), rows)
            slot = n % depth
            source = act_ref.at[some, h * half : (h + 1) * half]
            moves = [pltpu.make_async_copy(source, act.at[slot], sems.at[0, slot])]
            if h == 0:
                slot = n // 2 % 2
                moves.append(pltpu.make_async_copy(err_ref.at[some], err.at[slot], sems.at[1, slot]))
            return moves

        weights = (
            pltpu.make_async_copy(pa_ref, pa, wsems.at[0]),
            pltpu.make_async_copy(pe_ref, pe, wsems.at[1]),
        )
        for one in weights:
            one.start()
        for n in range(depth):
            for one in copies(n):
                one.start()
        for one in weights:
            one.wait()
        for n, (r, h) in enumerate(order):
            for one in copies(n):
                one.wait()
            some = slice((n // 2 % per) * rows, (n // 2 % per + 1) * rows)
            part = dot(act[n % depth], pa[h * half : (h + 1) * half], NN)
            if h == 0:
                outs[r][some, :rank] = part
                outs[r][some, rank:] = dot(err[n // 2 % 2], pe[...], NN)
            else:
                outs[r][some, :rank] += part
            if n + depth < len(order):
                for one in copies(n + depth):
                    one.start()

    return pl.pallas_call(
        body,
        out_shape=[shaped((own, 2 * rank), F32)] * n_w,
        in_specs=[SCALARS] + [pl.BlockSpec(memory_space=pl.ANY)] * 4,
        out_specs=[WHOLE] * n_w,
        scratch_shapes=[
            pltpu.VMEM(proj_acts.shape, BF16),
            pltpu.VMEM(proj_errs.shape, BF16),
            pltpu.VMEM((depth, rows, half), BF16),
            pltpu.VMEM((2, rows, feats_e), BF16),
            pltpu.SemaphoreType.DMA((2,)),
            pltpu.SemaphoreType.DMA((2, depth)),
        ],
        compiler_params=pltpu.CompilerParams(vmem_limit_bytes=18 * MIB),
        cost_estimate=BRIEF,
    )(ranks, activations, errors, proj_acts, proj_errs)


def gradients(ranks, parts):
    n_w = len(parts)
    tokens, both = parts[0].shape
    rank = both // 2
    seqs = tokens // SEQ_LEN
    lines = rank // n_w

    def body(ranks_ref, *refs):
        ins, outs, all_ref = refs[:n_w], refs[n_w : 2 * n_w], refs[2 * n_w]
        w = ranks_ref[0]
        total = ins[0][...]
        for ref in ins[1:]:
            total = total + ref[...]
        for j in range(seqs):
            rows = slice(j * SEQ_LEN, (j + 1) * SEQ_LEN)
            g = dot(total[rows, rank:], total[rows, :rank], TN, HIGHEST)
            all_ref[j] = (g / SEQ_LEN).astype(BF16)
        for r in range(n_w):
            some = pl.ds(pl.multiple_of((w ^ r) * lines, lines), lines)
            for j in range(seqs):
                outs[r][j] = all_ref[j, some, :]

    return call(
        body,
        [shaped((seqs, lines, rank), BF16)] * n_w,
        [ranks, *parts],
        limit=8,
        in_specs=[SCALARS] + [WHOLE] * n_w,
        out_specs=[WHOLE] * n_w,
        scratch_shapes=[pltpu.VMEM((seqs, rank, rank), BF16)],
    )


def join(ranks, pieces, mine, theirs):
    n_w = len(pieces)
    seqs, lines, rank = pieces[0].shape
    count, chunk = mine.shape[1:]
    group = n_w * seqs
    rows = lines * group
    blocks = chunk // rank

    def body(ranks_ref, *refs):
        ins, mine_ref, theirs_ref, out, order_ref = refs[:n_w], *refs[n_w:]
        for r in range(n_w):
            for j in range(seqs):
                order_ref[(ranks_ref[0] ^ r) * seqs + j] = ins[r][j].astype(F32)
        grads = jnp.swapaxes(order_ref[...], 0, 1).astype(BF16)
        out[:rows] = grads.reshape(rows, rank)
        total = (mine_ref[0] + theirs_ref[0].astype(F32)).astype(BF16)
        for b in range(blocks):
            out[rows + b * count : rows + (b + 1) * count] = total[:, b * rank : (b + 1) * rank]

    return call(
        body,
        shaped((rows + blocks * count, rank), BF16),
        [ranks, *pieces, mine, theirs],
        limit=8,
        in_specs=[SCALARS] + [WHOLE] * (n_w + 2),
        out_specs=WHOLE,
        scratch_shapes=[pltpu.VMEM((group, lines, rank), F32)],
    )


def first_product(ranks, fisher, rhs_t, n_w, n_s, parity):
    row_len, col_len = fisher.shape
    chunk = col_len // n_s
    count = rhs_t[0].shape[0]
    steps = n_s // 2
    shift = ridge_damp - center
    blocks = [(t, r) for t in range(steps) for r in range(n_w)]
    depth = min(8, len(blocks))

    def body(ranks_ref, fisher_ref, *refs):
        vec, (y_ref, keep_ref, held, sems) = refs[:n_w], refs[n_w:]
        w, s = ranks_ref[0], ranks_ref[1]

        def copy(n):
            t, r = blocks[n]
            rows = pl.ds(pl.multiple_of((w ^ r) * chunk, chunk), chunk)
            cols = pl.ds(pl.multiple_of((s ^ (2 * t + parity)) * chunk, chunk), chunk)
            slot = n % depth
            return pltpu.make_async_copy(fisher_ref.at[rows, cols], held.at[slot], sems.at[slot])

        for n in range(depth):
            copy(n).start()
        for n, (t, r) in enumerate(blocks):
            copy(n).wait()
            slot = n % depth
            keep_ref[t, r] = held[slot].astype(BF16)

            @pl.when(w * n_s + (s ^ (2 * t + parity)) == s * n_w + (w ^ r))
            def _():
                i = lax.broadcasted_iota(jnp.int32, (chunk, chunk), 0)
                j = lax.broadcasted_iota(jnp.int32, (chunk, chunk), 1)
                keep_ref[t, r] = (held[slot] + jnp.where(i == j, shift, 0.0)).astype(BF16)

            part = dot(vec[r][...], keep_ref[t, r], NN)
            if r == 0:
                y_ref[t] = part
            else:
                y_ref[t] += part
            if n + depth < len(blocks):
                copy(n + depth).start()

    return pl.pallas_call(
        body,
        out_shape=[
            shaped((steps, count, chunk), F32),
            pltpu.VMEM((steps, n_w, chunk, chunk), BF16),
        ],
        in_specs=[SCALARS, pl.BlockSpec(memory_space=pl.ANY)] + [WHOLE] * n_w,
        out_specs=[WHOLE, WHOLE],
        scratch_shapes=[
            pltpu.VMEM((depth, chunk, chunk), F32),
            pltpu.SemaphoreType.DMA((depth,)),
        ],
        compiler_params=pltpu.CompilerParams(vmem_limit_bytes=12 * MIB),
        cost_estimate=BRIEF,
    )(ranks, fisher, *rhs_t)


def fold(mine, theirs):
    left, count, chunk = mine.shape

    def body(mine_ref, theirs_ref, keep_ref, send_ref):
        for i in range(left):
            total = mine_ref[i] + theirs_ref[i].astype(F32)
            if i % 2 == 0:
                keep_ref[i // 2] = total
            else:
                send_ref[i // 2] = total.astype(BF16)

    half = (left // 2, count, chunk)
    return call(body, [shaped(half, F32), shaped(half, BF16)], [mine, theirs])


def halves(x):
    high = x.astype(BF16)
    return high, (x - high.astype(F32)).astype(BF16)


def panel(ranks, joined, rows_t, group):
    n_s = len(joined)
    n_w = len(rows_t)
    count, chunk = rows_t[0].shape
    rank = joined[0].shape[1]
    seqs = n_s * group
    per = chunk // rank
    rows = joined[0].shape[0] - per * count
    ratio = n_s // n_w

    def body(ranks_ref, *refs):
        in_refs, q_refs = refs[:n_s], refs[n_s : n_s + n_w]
        x_ref, both_ref, product_ref, out = refs[n_s + n_w :]
        w, s = ranks_ref[0], ranks_ref[1]
        both = jnp.zeros((seqs, count + seqs), F32)
        for p in range(n_s):
            for ii in range(per):
                lanes = slice(ii * rank, (ii + 1) * rank)
                x_ref[p, :count, lanes] = in_refs[p][rows + ii * count : rows + (ii + 1) * count]
                line = pl.ds(pl.multiple_of(((s ^ p) * per + ii) * group, group), group)
                for j in range(n_s):
                    at = pl.ds(pl.multiple_of(count + (s ^ j) * group, group), group)
                    x_ref[p, at, lanes] = in_refs[j][line, :]
            both = both + dot(x_ref[p, count:], x_ref[p], NT)
        both_ref[...] = both
        product = jnp.zeros((seqs, count), F32)
        for r in range(n_w):
            at = s ^ ((s % ratio) * n_w + (w ^ r))
            product = product + dot(x_ref[at, count:], q_refs[r][...], NT)
        product = jnp.where(s // ratio == w, product, 0.0)
        product_ref[...] = product
        out[0, :, : count + seqs], out[1, :, : count + seqs] = halves(both)
        out[0, :, count + seqs :], out[1, :, count + seqs :] = halves(product)

    args = [ranks, *joined, *rows_t]
    outs = [
        shaped((n_s, count + seqs, chunk), BF16),
        shaped((seqs, count + seqs), F32),
        shaped((seqs, count), F32),
        shaped((2, seqs, 2 * count + seqs), BF16),
    ]
    return call(
        body,
        outs,
        args,
        limit=12,
        in_specs=[SCALARS] + [WHOLE] * (len(args) - 1),
        out_specs=[WHOLE] * len(outs),
    )


def settle(both, product, others):
    wide = both.shape[1]

    def body(both_ref, product_ref, *refs):
        total, right = both_ref[...], product_ref[...]
        for ref in refs[:-2]:
            whole = ref[0].astype(F32) + ref[1].astype(F32)
            total = total + whole[:, :wide]
            right = right + whole[:, wide:]
        refs[-2][...] = total
        refs[-1][...] = right

    outs = [shaped(x.shape, F32) for x in (both, product)]
    return call(body, outs, [both, product, *others], limit=8)


def second_product(keep_even, keep_odd, x):
    _, n_w, chunk, _ = keep_even.shape
    n_s, wide, _ = x.shape

    def body(even_ref, odd_ref, x_ref, *outs):
        for r in range(n_w - 1, -1, -1):
            total = jnp.zeros((chunk, wide), F32)
            for p in range(n_s):
                block = even_ref[p // 2, r] if p % 2 == 0 else odd_ref[p // 2, r]
                total = total + dot(block, x_ref[p], NT)
            outs[r][...] = total.astype(outs[r].dtype)

    outs = [shaped((chunk, wide), F32)] + [shaped((chunk, wide), BF16)] * (n_w - 1)
    return call(
        body,
        outs,
        [keep_even, keep_odd, x],
        limit=12,
        in_specs=[WHOLE] * 3,
        out_specs=[WHOLE] * len(outs),
    )


def prepare(ranks, rhs, x_own, both, first, n_w, n_s):
    chunk, count = rhs.shape
    seqs = both.shape[0]
    local = seqs // (n_w * n_s)

    def body(ranks_ref, rhs_ref, x_ref, both_ref, first_in_ref, sol_ref, res_ref, score_ref, first_ref, coef_ref):
        w, s = ranks_ref[0], ranks_ref[1]
        first = first_in_ref[...] / seqs
        first_ref[...] = first
        second = both_ref[:, :count] + dot(both_ref[:, count:], first, NN, HIGHEST)
        second = second / seqs
        q = rhs_ref[...]
        g = x_ref[count:].astype(F32)
        once = x_ref[:count].astype(F32).T + dot(g, first, TN, HIGHEST)
        sol_ref[...] = lead * q - tail * once
        res_ref[...] = tail * dot(g, second, TN, HIGHEST) - fall * q
        coef_ref[...] = seqs * (lead * first - tail * second)
        for j in range(local):
            row = (w * n_s + s) * local + j
            score_ref[pl.ds(j, 1), :] = coef_ref[pl.ds(row, 1), :]

    args = [ranks, rhs, x_own, both, first]
    outs = [shaped((chunk, count), F32)] * 2
    outs += [shaped((local, count), F32), shaped((seqs, count), F32)]
    return call(
        body,
        outs,
        args,
        limit=8,
        in_specs=[SCALARS] + [WHOLE] * (len(args) - 1),
        out_specs=[WHOLE] * len(outs),
        scratch_shapes=[pltpu.VMEM((seqs, count), F32)],
    )


def finish(residual, first, own, others):
    count = residual.shape[1]

    def body(res_in_ref, first_ref, own_ref, *refs):
        total = own_ref[...]
        for ref in refs[:-1]:
            total = total + ref[...].astype(F32)
        total = total[:, :count] + dot(total[:, count:], first_ref[...], NN, HIGHEST)
        refs[-1][...] = res_in_ref[...] + tail * total

    return call(body, shaped(residual.shape, F32), [residual, first, own, *others], limit=8)


def turn(rhs):
    def body(rhs_ref, out_ref):
        out_ref[...] = rhs_ref[...].T.astype(BF16)

    return call(body, shaped(rhs.shape[::-1], BF16), [rhs], limit=8)


def on_device(activations, errors, proj_acts, proj_errs, fisher, queries):
    n_w = lax.axis_size("width")
    n_s = lax.axis_size("seq")
    ranks = jnp.stack([lax.axis_index("width"), lax.axis_index("seq")]).astype(jnp.int32)
    rhs = queries.reshape(queries.shape[1:])
    to_rows = [(b, (b % n_w) * n_s + b // n_w) for b in range(n_w * n_s)]

    rhs_t = turn(rhs)
    rows_t = [rhs_t] + [swap(rhs_t, "width", r) for r in range(1, n_w)]

    activations, errors, proj_acts, proj_errs, fisher = [
        pltpu.with_memory_space_constraint(x, pltpu.HBM)
        for x in (activations, errors, proj_acts, proj_errs, fisher)
    ]
    pieces = project(ranks, activations, errors, proj_acts, proj_errs, n_w)
    fisher, *pieces = lax.optimization_barrier((fisher, *pieces))
    pieces = [pieces[0]] + [swap(pieces[r], "width", r) for r in range(1, n_w)]

    theirs, keep_odd = first_product(ranks, fisher, rows_t, n_w, n_s, 1)
    theirs = swap(theirs, "seq", 1)
    mine, keep_even = first_product(ranks, fisher, rows_t, n_w, n_s, 0)
    keep, sent = fold(mine, theirs)
    sent = swap(sent, "seq", 2)
    keep, sent, *pieces = lax.optimization_barrier((keep, sent, *pieces))
    grads = gradients(ranks, pieces)
    group = n_w * grads[0].shape[0]
    bit = 4
    while keep.shape[0] > 1:
        keep, sent = fold(keep, sent)
        sent, *grads = lax.optimization_barrier((sent, *grads))
        sent = swap(sent, "seq", bit)
        bit *= 2
    grads = [grads[0]] + [swap(grads[r], "width", r) for r in range(1, n_w)]
    joined = {0: join(ranks, grads, keep, sent)}
    bit = n_s // 2
    while bit:
        joined |= {p | bit: swap(joined[p], "seq", bit) for p in list(joined)}
        bit //= 2
    joined = [joined[p] for p in range(n_s)]

    x, both, product, sent = panel(ranks, joined, rows_t, group)
    small = [swap(sent, "width", r) for r in range(1, n_w)]
    x_own = lax.ppermute(x[0], ("width", "seq"), to_rows)
    own, *sent = second_product(keep_even, keep_odd, x)
    sent = [swap(sent[r - 1], "width", r) for r in range(1, n_w)]
    x_own, *small = lax.optimization_barrier((x_own, *small))
    both, product = settle(both, product, small)
    bit = 1
    while bit < n_s:
        product = product + swap(product, "seq", bit)
        bit *= 2
    solution, residual, scores, first = prepare(ranks, rhs, x_own, both, product, n_w, n_s)
    residual = finish(residual, first, own, sent)
    return solution.reshape(queries.shape), residual.reshape(queries.shape), scores


def solution(mesh):
    placed = (
        P("seq", "width"),
        P("seq", "width"),
        P("width", None),
        P("width", None),
        P("seq", "width"),
        P("seq", "width", None),
    )
    return jax.shard_map(
        on_device,
        mesh=mesh,
        in_specs=placed,
        out_specs=(P("seq", "width", None), P("seq", "width", None), P(("width", "seq"), None)),
        check_vma=False,
    )
```

time: 393 us -> 117 us (0.30)
  waiting for transfers between devices: 243 us -> 43.2 us
  matrix products: 100 us -> 0 us
  Pallas kernels: 0 us -> 35.6 us
  starting transfers between devices: 9.59 us -> 36.3 us
  local copies, waits for them, and re-layouts: 17.1 us -> 0.97 us
  between operations: 15.6 us -> 0.84 us
  other arithmetic: 5.35 us -> 0.1 us
    dot_general x7 -> x0, matrix products: 100 us -> none  [the longest x2 61.9 us: apply_op(): jnp.dot(damped, col_block, precision=highest, preferred_element_type=jnp....]
    unnamed x8 -> x0, waiting for transfers between devices: 71.6 us -> none
    all_gather x3 -> x0, waiting for transfers between devices: 65.1 us -> none  [the longest x1 34.5 us: on_device(): gathered = lax.all_gather(seq_grads, ('width', 'seq'), axis=0, tiled=True)]
    reduce_scatter x3 -> x0, waiting for transfers between devices: 56.3 us -> none  [the longest x1 29.7 us: on_device(): lax.psum_scatter(jnp.concatenate([jnp.dot(activations, proj_acts, preferr...]
    all_to_all x2 -> x0, waiting for transfers between devices: 49.8 us -> none  [column_block(): lax.all_to_all(grouped, 'width', split_axis=0, concat_axis=2, tiled=True)]
    ppermute x0 -> x29, waiting for transfers between devices: none -> 43.2 us  [the longest x28 43.2 us: swap(): lax.ppermute(x, axis, [(i, i ^ k) for i in range(lax.axis_size(axis))])]
    ppermute x0 -> x29, starting transfers between devices: none -> 36.3 us  [the longest x28 35.6 us: swap(): lax.ppermute(x, axis, [(i, i ^ k) for i in range(lax.axis_size(axis))])]
    pallas_call x0 -> x13, Pallas kernels: none -> 35.6 us  [the longest x2 13.9 us: first_product(): pl.pallas_call(body, out_shape=[shaped((steps, count, chunk), F32), pltpu...]
  transfers between devices with their start and end apart: 9 -> 29, of which waited for: 8 -> 14; matrix products, arithmetic and copies ran while one was open for 11% -> 0% of each run, Pallas kernels for 0% -> 21%
where the time goes in v2:
time: 117 us
  waiting for transfers between devices  43.2 us (37%)
  starting transfers between devices  36.3 us (31%)
  Pallas kernels  35.6 us (30%)
    ppermute x28, waiting for transfers between devices, swap(): lax.ppermute(x, axis, [(i, i ^ k) for i in range(lax.axis_size(axis))])  43.2 us
    ppermute x28, starting transfers between devices, swap(): lax.ppermute(x, axis, [(i, i ^ k) for i in range(lax.axis_size(axis))])  35.6 us
    pallas_call x2, Pallas kernels, first_product(): pl.pallas_call(body, out_shape=[shaped((steps, count, chunk), F32), pltpu...  13.9 us
    pallas_call x10, Pallas kernels, call(): pl.pallas_call(body, out_shape=out, compiler_params=pltpu.CompilerParams(...  11.2 us
    pallas_call x1, Pallas kernels, project(): pl.pallas_call(body, out_shape=[shaped((own, 2 * rank), F32)] * n_w, in_s...  10.6 us
  transfers between devices with their start and end apart: 29, of which 14 were waited for; matrix products, arithmetic and copies ran while one was open for 0% of the time, Pallas kernels for 21%

profile of v2, /device:TPU:0, one launch (start us, length us, event | category | flops | bytes accessed | tf_op | source)
XLA Modules:
  0.0 117.0 jit_solution(7989120067707303984)
XLA Ops:
  0.6 0.0 copy-start
  0.6 0.9 copy-done
  1.6 0.1 shard_map.86.refs_0_.refs_8_
  1.7 4.0 %collective-permute-start.2 = (bf16[128,512]{1,0:T(8,128)(2,1)S(1)}, bf16[128,512]{1,0:T(8,128)(2,1)S(1)}, u32[]{:S(2)}, u32[]{:S(2)}) collective-permute-start(bf16[128,512]{1,0:T(8,128)(2,1)S(1)} %shard_map.86.refs_0_.refs_8_), channel_id=1, source_target_pairs={{0,24},{8,16},{16,8},{24,0},{1,25},{9,17},{17,9},{25,1},{2,26},{10... | collective-permute-start | bytes 393224 | tf_op jit(solution)/shard_map/ppermute | solution.py:45
  5.7 0.5 collective-permute-start.1
  6.2 0.1 collective-permute-start
  6.3 0.1 pad_add_fusion.ranks_ref
  6.4 10.6 %shard_map.85 = (f32[256,256]{1,0:T(8,128)S(1)}, f32[256,256]{1,0:T(8,128)S(1)}, f32[256,256]{1,0:T(8,128)S(1)}, f32[256,256]{1,0:T(8,128)S(1)}) custom-call(s32[2]{0:T(128)S(1)} %pad_add_fusion.ranks_ref, bf16[1024,7168]{1,0:T(8,128)(2,1)} %act_ref.1, bf16[1024,2048]{1,0:T(8,128)(2,1)} %err_ref.1, bf16[7168,128]{1,0:T(8,128)(2,1)} %pa_ref.1, ...), custom_call_target="tpu_custom_call" | custom-call | flops 1 | bytes 1 | tf_op jit(solution)/shard_map/pallas_call | solution.py:110
  16.9 0.0 collective-permute-done.2.refs_3_.refs_11_
  17.0 0.0 collective-permute-done.1.refs_2_.refs_10_
  17.0 7.0 %shard_map.88 = (f32[4,128,512]{2,1,0:T(8,128)S(1)}, bf16[4,4,512,512]{3,2,1,0:T(8,128)(2,1)S(1)}) custom-call(s32[2]{0:T(128)S(1)} %pad_add_fusion.ranks_ref, f32[2048,4096]{1,0:T(8,128)} %fisher_ref.1, bf16[128,512]{1,0:T(8,128)(2,1)S(1)} %shard_map.86.refs_0_.refs_8_, bf16[128,512]{1,0:T(8,128)(2,1)S(1)} %collective-permute-done.refs_1_.refs_9_, ...), custom_call_target="tpu_custom_call" | custom-call | flops 1 | bytes 1 | tf_op jit(solution)/shard_map/pallas_call | solution.py:232
  23.9 0.1 collective-permute-start.3
  24.0 1.9 %collective-permute-start.5 = (f32[256,256]{1,0:T(8,128)S(1)}, f32[256,256]{1,0:T(8,128)S(1)}, u32[]{:S(2)}, u32[]{:S(2)}) collective-permute-start(f32[256,256]{1,0:T(8,128)S(1)} %get-tuple-element.63), channel_id=1, source_target_pairs={{0,8},{8,0},{16,24},{24,16},{1,9},{9,1},{17,25},{25,17},{2,10},{10... | collective-permute-start | bytes 786440 | tf_op jit(solution)/shard_map/ppermute | solution.py:45
  26.0 1.5 %collective-permute-start.6 = (f32[256,256]{1,0:T(8,128)S(1)}, f32[256,256]{1,0:T(8,128)S(1)}, u32[]{:S(2)}, u32[]{:S(2)}) collective-permute-start(f32[256,256]{1,0:T(8,128)S(1)} %get-tuple-element.64), channel_id=1, source_target_pairs={{0,16},{8,24},{16,0},{24,8},{1,17},{9,25},{17,1},{25,9},{2,18},{10... | collective-permute-start | bytes 786440 | tf_op jit(solution)/shard_map/ppermute | solution.py:45
  27.5 0.1 collective-permute-start.7
  27.6 6.9 %shard_map.87 = (f32[4,128,512]{2,1,0:T(8,128)S(1)}, bf16[4,4,512,512]{3,2,1,0:T(8,128)(2,1)S(1)}) custom-call(s32[2]{0:T(128)S(1)} %pad_add_fusion.ranks_ref, f32[2048,4096]{1,0:T(8,128)} %fisher_ref.1, bf16[128,512]{1,0:T(8,128)(2,1)S(1)} %shard_map.86.refs_0_.refs_8_, bf16[128,512]{1,0:T(8,128)(2,1)S(1)} %collective-permute-done.refs_1_.refs_9_, ...), custom_call_target="tpu_custom_call" | custom-call | flops 1 | bytes 1 | tf_op jit(solution)/shard_map/pallas_call | solution.py:232
  34.5 0.1 shard_map.89
  34.6 2.0 %collective-permute-start.4 = (bf16[2,128,512]{2,1,0:T(8,128)(2,1)S(1)}, bf16[2,128,512]{2,1,0:T(8,128)(2,1)S(1)}, u32[]{:S(2)}, u32[]{:S(2)}) collective-permute-start(bf16[2,128,512]{2,1,0:T(8,128)(2,1)S(1)} %get-tuple-element.61), channel_id=1, source_target_pairs={{0,2},{1,3},{2,0},{3,1},{4,6},{5,7},{6,4},{7,5},{8,10},{9,11},{10,... | collective-permute-start | bytes 786440 | tf_op jit(solution)/shard_map/ppermute | solution.py:45
  36.7 0.0 collective-permute-done.5.refs_1_
  36.7 3.3 %collective-permute-done.6.refs_2_ = f32[256,256]{1,0:T(8,128)S(1)} collective-permute-done((f32[256,256]{1,0:T(8,128)S(1)}, f32[256,256]{1,0:T(8,128)S(1)}, u32[]{:S(2)}, u32[]{:S(2)}) %collective-permute-start.6) | collective-permute-done | bytes 262176 | tf_op jit(solution)/shard_map/ppermute | solution.py:45
  40.0 2.8 %collective-permute-done.4.theirs_ref = bf16[2,128,512]{2,1,0:T(8,128)(2,1)S(1)} collective-permute-done((bf16[2,128,512]{2,1,0:T(8,128)(2,1)S(1)}, bf16[2,128,512]{2,1,0:T(8,128)(2,1)S(1)}, u32[]{:S(2)}, u32[]{:S(2)}) %collective-permute-start.4) | collective-permute-done | bytes 262176 | tf_op jit(solution)/shard_map/ppermute | solution.py:45
  42.8 0.1 shard_map.90
  42.8 1.0 shard_map.91
  43.8 2.8 %collective-permute-start.11 = (bf16[1,128,512]{2,1,0:T(8,128)(2,1)S(1)}, bf16[1,128,512]{2,1,0:T(8,128)(2,1)S(1)}, u32[]{:S(2)}, u32[]{:S(2)}) collective-permute-start(bf16[1,128,512]{2,1,0:T(8,128)(2,1)S(1)} %get-tuple-element.82), channel_id=1, source_target_pairs={{0,4},{1,5},{2,6},{3,7},{4,0},{5,1},{6,2},{7,3},{8,12},{9,13},{10,... | collective-permute-start | bytes 393224 | tf_op jit(solution)/shard_map/ppermute | solution.py:45
  46.6 1.5 %collective-permute-start.8 = (bf16[4,32,128]{2,1,0:T(8,128)(2,1)S(1)}, bf16[4,32,128]{2,1,0:T(8,128)(2,1)S(1)}, u32[]{:S(2)}, u32[]{:S(2)}) collective-permute-start(bf16[4,32,128]{2,1,0:T(8,128)(2,1)S(1)} %get-tuple-element.78), channel_id=1, source_target_pairs={{0,8},{8,0},{16,24},{24,16},{1,9},{9,1},{17,25},{25,17},{2,10},{10... | collective-permute-start | bytes 98312 | tf_op jit(solution)/shard_map/ppermute | solution.py:45
  48.1 1.5 %collective-permute-start.9 = (bf16[4,32,128]{2,1,0:T(8,128)(2,1)S(1)}, bf16[4,32,128]{2,1,0:T(8,128)(2,1)S(1)}, u32[]{:S(2)}, u32[]{:S(2)}) collective-permute-start(bf16[4,32,128]{2,1,0:T(8,128)(2,1)S(1)} %get-tuple-element.79), channel_id=1, source_target_pairs={{0,16},{8,24},{16,0},{24,8},{1,17},{9,25},{17,1},{25,9},{2,18},{10... | collective-permute-start | bytes 98312 | tf_op jit(solution)/shard_map/ppermute | solution.py:45
  49.6 0.5 collective-permute-start.10
  50.1 0.6 collective-permute-done.8.refs_1_
  50.7 1.3 %collective-permute-done.9.refs_2_ = bf16[4,32,128]{2,1,0:T(8,128)(2,1)S(1)} collective-permute-done((bf16[4,32,128]{2,1,0:T(8,128)(2,1)S(1)}, bf16[4,32,128]{2,1,0:T(8,128)(2,1)S(1)}, u32[]{:S(2)}, u32[]{:S(2)}) %collective-permute-start.9) | collective-permute-done | bytes 32800 | tf_op jit(solution)/shard_map/ppermute | solution.py:45
  52.0 2.4 %collective-permute-done.10.refs_3_ = bf16[4,32,128]{2,1,0:T(8,128)(2,1)S(1)} collective-permute-done((bf16[4,32,128]{2,1,0:T(8,128)(2,1)S(1)}, bf16[4,32,128]{2,1,0:T(8,128)(2,1)S(1)}, u32[]{:S(2)}, u32[]{:S(2)}) %collective-permute-start.10) | collective-permute-done | bytes 32800 | tf_op jit(solution)/shard_map/ppermute | solution.py:45
  54.4 0.0 collective-permute-done.11.refs_5_
  54.4 0.6 shard_map.92.refs_0_
  55.1 0.4 collective-permute-start.15
  55.5 1.6 %collective-permute-start.13 = (bf16[1024,128]{1,0:T(8,128)(2,1)S(1)}, bf16[1024,128]{1,0:T(8,128)(2,1)S(1)}, u32[]{:S(2)}, u32[]{:S(2)}) collective-permute-start(bf16[1024,128]{1,0:T(8,128)(2,1)S(1)} %shard_map.92.refs_0_), channel_id=1, source_target_pairs={{0,2},{1,3},{2,0},{3,1},{4,6},{5,7},{6,4},{7,5},{8,10},{9,11},{10,... | collective-permute-start | bytes 786440 | tf_op jit(solution)/shard_map/ppermute | solution.py:45
  57.1 10.1 %collective-permute-done.15.refs_4_ = bf16[1024,128]{1,0:T(8,128)(2,1)S(1)} collective-permute-done((bf16[1024,128]{1,0:T(8,128)(2,1)S(1)}, bf16[1024,128]{1,0:T(8,128)(2,1)S(1)}, u32[]{:S(2)}, u32[]{:S(2)}) %collective-permute-start.15) | collective-permute-done | bytes 262176 | tf_op jit(solution)/shard_map/ppermute | solution.py:45
  67.1 0.0 collective-permute-start.17
  67.1 0.5 collective-permute-start.16
  67.6 0.0 collective-permute-start.14
  67.6 6.8 %collective-permute-done.17.refs_6_ = bf16[1024,128]{1,0:T(8,128)(2,1)S(1)} collective-permute-done((bf16[1024,128]{1,0:T(8,128)(2,1)S(1)}, bf16[1024,128]{1,0:T(8,128)(2,1)S(1)}, u32[]{:S(2)}, u32[]{:S(2)}) %collective-permute-start.17) | collective-permute-done | bytes 262176 | tf_op jit(solution)/shard_map/ppermute | solution.py:45
  74.4 0.0 collective-permute-start.18
  74.4 0.0 collective-permute-done.12.refs_1_
  74.4 0.0 collective-permute-done.16.refs_5_
  74.4 1.5 %collective-permute-done.18.refs_7_ = bf16[1024,128]{1,0:T(8,128)(2,1)S(1)} collective-permute-done((bf16[1024,128]{1,0:T(8,128)(2,1)S(1)}, bf16[1024,128]{1,0:T(8,128)(2,1)S(1)}, u32[]{:S(2)}, u32[]{:S(2)}) %collective-permute-start.18) | collective-permute-done | bytes 262176 | tf_op jit(solution)/shard_map/ppermute | solution.py:45
  76.0 1.7 %shard_map.93 = (bf16[8,256,512]{2,1,0:T(8,128)(2,1)S(1)}, f32[128,256]{1,0:T(8,128)S(1)}, f32[128,128]{1,0:T(8,128)S(1)}, bf16[2,128,384]{2,1,0:T(8,128)(2,1)S(1)}) custom-call(s32[2]{0:T(128)S(1)} %pad_add_fusion.ranks_ref, bf16[1024,128]{1,0:T(8,128)(2,1)S(1)} %shard_map.92.refs_0_, bf16[1024,128]{1,0:T(8,128)(2,1)S(1)} %collective-permute-done.12.refs_1_, ...), custom_call_target="tpu_custom_call" | custom-call | flops 1 | bytes 1 | tf_op jit(solution)/shard_map/pallas_call | solution.py:49
  77.7 0.7 collective-permute-start.19
  78.4 4.9 %collective-permute-start.22 = (bf16[2,128,384]{2,1,0:T(8,128)(2,1)S(1)}, bf16[2,128,384]{2,1,0:T(8,128)(2,1)S(1)}, u32[]{:S(2)}, u32[]{:S(2)}) collective-permute-start(bf16[2,128,384]{2,1,0:T(8,128)(2,1)S(1)} %get-tuple-element.84), channel_id=1, source_target_pairs={{0,24},{8,16},{16,8},{24,0},{1,25},{9,17},{17,9},{25,1},{2,26},{10... | collective-permute-start | bytes 589832 | tf_op jit(solution)/shard_map/ppermute | solution.py:45
  83.3 0.0 collective-permute-start.21
  83.3 0.6 collective-permute-start.20
  83.9 4.5 %shard_map.96 = (f32[512,256]{1,0:T(8,128)S(1)}, bf16[512,256]{1,0:T(8,128)(2,1)S(1)}, bf16[512,256]{1,0:T(8,128)(2,1)S(1)}, bf16[512,256]{1,0:T(8,128)(2,1)S(1)}) custom-call(bf16[4,4,512,512]{3,2,1,0:T(8,128)(2,1)S(1)} %get-tuple-element.96.even_ref, bf16[4,4,512,512]{3,2,1,0:T(8,128)(2,1)S(1)} %get-tuple-element.97.odd_ref, ...), custom_call_target="tpu_custom_call" | custom-call | flops 1 | bytes 1 | tf_op jit(solution)/shard_map/pallas_call | solution.py:49
  88.5 1.5 %collective-permute-start.26 = (bf16[512,256]{1,0:T(8,128)(2,1)S(1)}, bf16[512,256]{1,0:T(8,128)(2,1)S(1)}, u32[]{:S(2)}, u32[]{:S(2)}) collective-permute-start(bf16[512,256]{1,0:T(8,128)(2,1)S(1)} %get-tuple-element.99), channel_id=1, source_target_pairs={{0,8},{8,0},{16,24},{24,16},{1,9},{9,1},{17,25},{25,17},{2,10},{10... | collective-permute-start | bytes 786440 | tf_op jit(solution)/shard_map/ppermute | solution.py:45
  89.9 0.7 collective-permute-done.22.refs_2_
  90.6 1.4 %collective-permute-start.27 = (bf16[512,256]{1,0:T(8,128)(2,1)S(1)}, bf16[512,256]{1,0:T(8,128)(2,1)S(1)}, u32[]{:S(2)}, u32[]{:S(2)}) collective-permute-start(bf16[512,256]{1,0:T(8,128)(2,1)S(1)} %get-tuple-element.100), channel_id=1, source_target_pairs={{0,16},{8,24},{16,0},{24,8},{1,17},{9,25},{17,1},{25,9},{2,18},{10... | collective-permute-start | bytes 786440 | tf_op jit(solution)/shard_map/ppermute | solution.py:45
  92.0 1.6 %collective-permute-done.21.refs_1_ = bf16[2,128,384]{2,1,0:T(8,128)(2,1)S(1)} collective-permute-done((bf16[2,128,384]{2,1,0:T(8,128)(2,1)S(1)}, bf16[2,128,384]{2,1,0:T(8,128)(2,1)S(1)}, u32[]{:S(2)}, u32[]{:S(2)}) %collective-permute-start.21) | collective-permute-done | bytes 196640 | tf_op jit(solution)/shard_map/ppermute | solution.py:45
  93.6 0.8 collective-permute-start.28
  94.4 3.3 %collective-permute-done.20.refs_0_ = bf16[2,128,384]{2,1,0:T(8,128)(2,1)S(1)} collective-permute-done((bf16[2,128,384]{2,1,0:T(8,128)(2,1)S(1)}, bf16[2,128,384]{2,1,0:T(8,128)(2,1)S(1)}, u32[]{:S(2)}, u32[]{:S(2)}) %collective-permute-start.20) | collective-permute-done | bytes 196640 | tf_op jit(solution)/shard_map/ppermute | solution.py:45
  97.8 0.1 shard_map.94
  97.8 4.2 %collective-permute-start.23 = (f32[128,128]{1,0:T(8,128)S(1)}, f32[128,128]{1,0:T(8,128)S(1)}, u32[]{:S(2)}, u32[]{:S(2)}) collective-permute-start(f32[128,128]{1,0:T(8,128)S(1)} %get-tuple-element.92), channel_id=1, source_target_pairs={{0,1},{1,0},{2,3},{3,2},{4,5},{5,4},{6,7},{7,6},{8,9},{9,8},{10,11... | collective-permute-start | bytes 196616 | tf_op jit(solution)/shard_map/ppermute | solution.py:45
  102.1 0.9 collective-permute-done.23
  103.0 3.1 %collective-permute-start.24 = (f32[128,128]{1,0:T(8,128)S(1)}, f32[128,128]{1,0:T(8,128)S(1)}, u32[]{:S(2)}, u32[]{:S(2)}) collective-permute-start(f32[128,128]{1,0:T(8,128)S(1)} %add.9), channel_id=1, source_target_pairs={{0,2},{1,3},{2,0},{3,1},{4,6},{5,7},{6,4},{7,5},{8,10},{9,11},{10,... | collective-permute-start | bytes 196616 | tf_op jit(solution)/shard_map/ppermute | solution.py:45
  106.1 2.4 %collective-permute-done.24 = f32[128,128]{1,0:T(8,128)S(1)} collective-permute-done((f32[128,128]{1,0:T(8,128)S(1)}, f32[128,128]{1,0:T(8,128)S(1)}, u32[]{:S(2)}, u32[]{:S(2)}) %collective-permute-start.24) | collective-permute-done | bytes 65568 | tf_op jit(solution)/shard_map/ppermute | solution.py:45
  108.5 0.1 collective-permute-start.25
  108.6 5.5 %collective-permute-done.25 = f32[128,128]{1,0:T(8,128)S(1)} collective-permute-done((f32[128,128]{1,0:T(8,128)S(1)}, f32[128,128]{1,0:T(8,128)S(1)}, u32[]{:S(2)}, u32[]{:S(2)}) %collective-permute-start.25) | collective-permute-done | bytes 65568 | tf_op jit(solution)/shard_map/ppermute | solution.py:45
  114.1 1.9 %shard_map.95 = (f32[512,128]{1,0:T(8,128)}, f32[512,128]{1,0:T(8,128)S(1)}, f32[4,128]{1,0:T(4,128)}, f32[128,128]{1,0:T(8,128)S(1)}) custom-call(s32[2]{0:T(128)S(1)} %pad_add_fusion.ranks_ref, f32[512,128]{1,0:T(8,128)S(1)} %bitcast.8, bf16[256,512]{1,0:T(8,128)(2,1)S(1)} %collective-permute-done.19.x_ref, f32[128,256]{1,0:T(8,128)S(1)} %get-tuple-element.91.both_ref, ...), custom_call_target="tpu_custom_call" | custom-call | flops 1 | bytes 1 | tf_op jit(solution)/shard_map/pallas_call | solution.py:49
  115.9 1.1 shard_map.97
  (16 shorter events, 0.1 us)
Async XLA Ops:
  0.6 1.0 copy-start
  1.7 15.3 %collective-permute-start.2 = (bf16[128,512]{1,0:T(8,128)(2,1)S(1)}, bf16[128,512]{1,0:T(8,128)(2,1)S(1)}, u32[]{:S(2)}, u32[]{:S(2)}) collective-permute-start(bf16[128,512]{1,0:T(8,128)(2,1)S(1)} %shard_map.86.refs_0_.refs_8_), channel_id=1, source_target_pairs={{0,24},{8,16},{16,8},{24,0},{1,25},{9,17},{17,9},{25,1},{2,26},{10... | collective-permute-start | bytes 393224 | tf_op jit(solution)/shard_map/ppermute | solution.py:45
  5.7 11.3 %collective-permute-start.1 = (bf16[128,512]{1,0:T(8,128)(2,1)S(1)}, bf16[128,512]{1,0:T(8,128)(2,1)S(1)}, u32[]{:S(2)}, u32[]{:S(2)}) collective-permute-start(bf16[128,512]{1,0:T(8,128)(2,1)S(1)} %shard_map.86.refs_0_.refs_8_), channel_id=1, source_target_pairs={{0,16},{8,24},{16,0},{24,8},{1,17},{9,25},{17,1},{25,9},{2,18},{10... | collective-permute-start | bytes 393224 | tf_op jit(solution)/shard_map/ppermute | solution.py:45
  6.2 10.8 %collective-permute-start = (bf16[128,512]{1,0:T(8,128)(2,1)S(1)}, bf16[128,512]{1,0:T(8,128)(2,1)S(1)}, u32[]{:S(2)}, u32[]{:S(2)}) collective-permute-start(bf16[128,512]{1,0:T(8,128)(2,1)S(1)} %shard_map.86.refs_0_.refs_8_), channel_id=1, source_target_pairs={{0,8},{8,0},{16,24},{24,16},{1,9},{9,1},{17,25},{25,17},{2,10},{10... | collective-permute-start | bytes 393224 | tf_op jit(solution)/shard_map/ppermute | solution.py:45
  23.9 10.6 %collective-permute-start.3 = (f32[4,128,512]{2,1,0:T(8,128)S(1)}, f32[4,128,512]{2,1,0:T(8,128)S(1)}, u32[]{:S(2)}, u32[]{:S(2)}) collective-permute-start(f32[4,128,512]{2,1,0:T(8,128)S(1)} %get-tuple-element.59), channel_id=1, source_target_pairs={{0,1},{1,0},{2,3},{3,2},{4,5},{5,4},{6,7},{7,6},{8,9},{9,8},{10,11... | collective-permute-start | bytes 3145736 | tf_op jit(solution)/shard_map/ppermute | solution.py:45
  24.0 12.7 %collective-permute-start.5 = (f32[256,256]{1,0:T(8,128)S(1)}, f32[256,256]{1,0:T(8,128)S(1)}, u32[]{:S(2)}, u32[]{:S(2)}) collective-permute-start(f32[256,256]{1,0:T(8,128)S(1)} %get-tuple-element.63), channel_id=1, source_target_pairs={{0,8},{8,0},{16,24},{24,16},{1,9},{9,1},{17,25},{25,17},{2,10},{10... | collective-permute-start | bytes 786440 | tf_op jit(solution)/shard_map/ppermute | solution.py:45
  26.0 14.0 %collective-permute-start.6 = (f32[256,256]{1,0:T(8,128)S(1)}, f32[256,256]{1,0:T(8,128)S(1)}, u32[]{:S(2)}, u32[]{:S(2)}) collective-permute-start(f32[256,256]{1,0:T(8,128)S(1)} %get-tuple-element.64), channel_id=1, source_target_pairs={{0,16},{8,24},{16,0},{24,8},{1,17},{9,25},{17,1},{25,9},{2,18},{10... | collective-permute-start | bytes 786440 | tf_op jit(solution)/shard_map/ppermute | solution.py:45
  27.5 12.5 %collective-permute-start.7 = (f32[256,256]{1,0:T(8,128)S(1)}, f32[256,256]{1,0:T(8,128)S(1)}, u32[]{:S(2)}, u32[]{:S(2)}) collective-permute-start(f32[256,256]{1,0:T(8,128)S(1)} %get-tuple-element.65), channel_id=1, source_target_pairs={{0,24},{8,16},{16,8},{24,0},{1,25},{9,17},{17,9},{25,1},{2,26},{10... | collective-permute-start | bytes 786440 | tf_op jit(solution)/shard_map/ppermute | solution.py:45
  34.6 8.1 %collective-permute-start.4 = (bf16[2,128,512]{2,1,0:T(8,128)(2,1)S(1)}, bf16[2,128,512]{2,1,0:T(8,128)(2,1)S(1)}, u32[]{:S(2)}, u32[]{:S(2)}) collective-permute-start(bf16[2,128,512]{2,1,0:T(8,128)(2,1)S(1)} %get-tuple-element.61), channel_id=1, source_target_pairs={{0,2},{1,3},{2,0},{3,1},{4,6},{5,7},{6,4},{7,5},{8,10},{9,11},{10,... | collective-permute-start | bytes 786440 | tf_op jit(solution)/shard_map/ppermute | solution.py:45
  43.8 10.6 %collective-permute-start.11 = (bf16[1,128,512]{2,1,0:T(8,128)(2,1)S(1)}, bf16[1,128,512]{2,1,0:T(8,128)(2,1)S(1)}, u32[]{:S(2)}, u32[]{:S(2)}) collective-permute-start(bf16[1,128,512]{2,1,0:T(8,128)(2,1)S(1)} %get-tuple-element.82), channel_id=1, source_target_pairs={{0,4},{1,5},{2,6},{3,7},{4,0},{5,1},{6,2},{7,3},{8,12},{9,13},{10,... | collective-permute-start | bytes 393224 | tf_op jit(solution)/shard_map/ppermute | solution.py:45
  46.6 4.1 %collective-permute-start.8 = (bf16[4,32,128]{2,1,0:T(8,128)(2,1)S(1)}, bf16[4,32,128]{2,1,0:T(8,128)(2,1)S(1)}, u32[]{:S(2)}, u32[]{:S(2)}) collective-permute-start(bf16[4,32,128]{2,1,0:T(8,128)(2,1)S(1)} %get-tuple-element.78), channel_id=1, source_target_pairs={{0,8},{8,0},{16,24},{24,16},{1,9},{9,1},{17,25},{25,17},{2,10},{10... | collective-permute-start | bytes 98312 | tf_op jit(solution)/shard_map/ppermute | solution.py:45
  48.1 3.9 %collective-permute-start.9 = (bf16[4,32,128]{2,1,0:T(8,128)(2,1)S(1)}, bf16[4,32,128]{2,1,0:T(8,128)(2,1)S(1)}, u32[]{:S(2)}, u32[]{:S(2)}) collective-permute-start(bf16[4,32,128]{2,1,0:T(8,128)(2,1)S(1)} %get-tuple-element.79), channel_id=1, source_target_pairs={{0,16},{8,24},{16,0},{24,8},{1,17},{9,25},{17,1},{25,9},{2,18},{10... | collective-permute-start | bytes 98312 | tf_op jit(solution)/shard_map/ppermute | solution.py:45
  49.6 4.8 %collective-permute-start.10 = (bf16[4,32,128]{2,1,0:T(8,128)(2,1)S(1)}, bf16[4,32,128]{2,1,0:T(8,128)(2,1)S(1)}, u32[]{:S(2)}, u32[]{:S(2)}) collective-permute-start(bf16[4,32,128]{2,1,0:T(8,128)(2,1)S(1)} %get-tuple-element.80), channel_id=1, source_target_pairs={{0,24},{8,16},{16,8},{24,0},{1,25},{9,17},{17,9},{25,1},{2,26},{10... | collective-permute-start | bytes 98312 | tf_op jit(solution)/shard_map/ppermute | solution.py:45
  55.1 12.0 %collective-permute-start.15 = (bf16[1024,128]{1,0:T(8,128)(2,1)S(1)}, bf16[1024,128]{1,0:T(8,128)(2,1)S(1)}, u32[]{:S(2)}, u32[]{:S(2)}) collective-permute-start(bf16[1024,128]{1,0:T(8,128)(2,1)S(1)} %shard_map.92.refs_0_), channel_id=1, source_target_pairs={{0,4},{1,5},{2,6},{3,7},{4,0},{5,1},{6,2},{7,3},{8,12},{9,13},{10,... | collective-permute-start | bytes 786440 | tf_op jit(solution)/shard_map/ppermute | solution.py:45
  55.5 12.2 %collective-permute-start.13 = (bf16[1024,128]{1,0:T(8,128)(2,1)S(1)}, bf16[1024,128]{1,0:T(8,128)(2,1)S(1)}, u32[]{:S(2)}, u32[]{:S(2)}) collective-permute-start(bf16[1024,128]{1,0:T(8,128)(2,1)S(1)} %shard_map.92.refs_0_), channel_id=1, source_target_pairs={{0,2},{1,3},{2,0},{3,1},{4,6},{5,7},{6,4},{7,5},{8,10},{9,11},{10,... | collective-permute-start | bytes 786440 | tf_op jit(solution)/shard_map/ppermute | solution.py:45
  67.1 7.3 %collective-permute-start.17 = (bf16[1024,128]{1,0:T(8,128)(2,1)S(1)}, bf16[1024,128]{1,0:T(8,128)(2,1)S(1)}, u32[]{:S(2)}, u32[]{:S(2)}) collective-permute-start(bf16[1024,128]{1,0:T(8,128)(2,1)S(1)} %collective-permute-done.15.refs_4_), channel_id=1, source_target_pairs={{0,2},{1,3},{2,0},{3,1},{4,6},{5,7},{6,4},{7,5},{8,10},{9,11},{10,... | collective-permute-start | bytes 786440 | tf_op jit(solution)/shard_map/ppermute | solution.py:45
  67.1 7.3 %collective-permute-start.12 = (bf16[1024,128]{1,0:T(8,128)(2,1)S(1)}, bf16[1024,128]{1,0:T(8,128)(2,1)S(1)}, u32[]{:S(2)}, u32[]{:S(2)}) collective-permute-start(bf16[1024,128]{1,0:T(8,128)(2,1)S(1)} %shard_map.92.refs_0_), channel_id=1, source_target_pairs={{0,1},{1,0},{2,3},{3,2},{4,5},{5,4},{6,7},{7,6},{8,9},{9,8},{10,11... | collective-permute-start | bytes 786440 | tf_op jit(solution)/shard_map/ppermute | solution.py:45
  67.1 7.3 %collective-permute-start.16 = (bf16[1024,128]{1,0:T(8,128)(2,1)S(1)}, bf16[1024,128]{1,0:T(8,128)(2,1)S(1)}, u32[]{:S(2)}, u32[]{:S(2)}) collective-permute-start(bf16[1024,128]{1,0:T(8,128)(2,1)S(1)} %collective-permute-done.15.refs_4_), channel_id=1, source_target_pairs={{0,1},{1,0},{2,3},{3,2},{4,5},{5,4},{6,7},{7,6},{8,9},{9,8},{10,11... | collective-permute-start | bytes 786440 | tf_op jit(solution)/shard_map/ppermute | solution.py:45
  67.6 6.8 %collective-permute-start.14 = (bf16[1024,128]{1,0:T(8,128)(2,1)S(1)}, bf16[1024,128]{1,0:T(8,128)(2,1)S(1)}, u32[]{:S(2)}, u32[]{:S(2)}) collective-permute-start(bf16[1024,128]{1,0:T(8,128)(2,1)S(1)} %collective-permute-done.13.refs_2_), channel_id=1, source_target_pairs={{0,1},{1,0},{2,3},{3,2},{4,5},{5,4},{6,7},{7,6},{8,9},{9,8},{10,11... | collective-permute-start | bytes 786440 | tf_op jit(solution)/shard_map/ppermute | solution.py:45
  74.4 1.5 %collective-permute-start.18 = (bf16[1024,128]{1,0:T(8,128)(2,1)S(1)}, bf16[1024,128]{1,0:T(8,128)(2,1)S(1)}, u32[]{:S(2)}, u32[]{:S(2)}) collective-permute-start(bf16[1024,128]{1,0:T(8,128)(2,1)S(1)} %collective-permute-done.17.refs_6_), channel_id=1, source_target_pairs={{0,1},{1,0},{2,3},{3,2},{4,5},{5,4},{6,7},{7,6},{8,9},{9,8},{10,11... | collective-permute-start | bytes 786440 | tf_op jit(solution)/shard_map/ppermute | solution.py:45
  77.7 20.0 %collective-permute-start.19 = (bf16[256,512]{1,0:T(8,128)(2,1)S(1)}, bf16[256,512]{1,0:T(8,128)(2,1)S(1)}, u32[]{:S(2)}, u32[]{:S(2)}) collective-permute-start(bf16[256,512]{1,0:T(8,128)(2,1)S(1)} %slice_bitcast_fusion), channel_id=1, source_target_pairs={{0,0},{1,8},{2,16},{3,24},{4,1},{5,9},{6,17},{7,25},{8,2},{9,10},{... | collective-permute-start | bytes 786440 | tf_op jit(solution)/shard_map/ppermute | solution.py:456
  78.4 12.2 %collective-permute-start.22 = (bf16[2,128,384]{2,1,0:T(8,128)(2,1)S(1)}, bf16[2,128,384]{2,1,0:T(8,128)(2,1)S(1)}, u32[]{:S(2)}, u32[]{:S(2)}) collective-permute-start(bf16[2,128,384]{2,1,0:T(8,128)(2,1)S(1)} %get-tuple-element.84), channel_id=1, source_target_pairs={{0,24},{8,16},{16,8},{24,0},{1,25},{9,17},{17,9},{25,1},{2,26},{10... | collective-permute-start | bytes 589832 | tf_op jit(solution)/shard_map/ppermute | solution.py:45
  83.3 10.3 %collective-permute-start.21 = (bf16[2,128,384]{2,1,0:T(8,128)(2,1)S(1)}, bf16[2,128,384]{2,1,0:T(8,128)(2,1)S(1)}, u32[]{:S(2)}, u32[]{:S(2)}) collective-permute-start(bf16[2,128,384]{2,1,0:T(8,128)(2,1)S(1)} %get-tuple-element.84), channel_id=1, source_target_pairs={{0,16},{8,24},{16,0},{24,8},{1,17},{9,25},{17,1},{25,9},{2,18},{10... | collective-permute-start | bytes 589832 | tf_op jit(solution)/shard_map/ppermute | solution.py:45
  83.3 14.4 %collective-permute-start.20 = (bf16[2,128,384]{2,1,0:T(8,128)(2,1)S(1)}, bf16[2,128,384]{2,1,0:T(8,128)(2,1)S(1)}, u32[]{:S(2)}, u32[]{:S(2)}) collective-permute-start(bf16[2,128,384]{2,1,0:T(8,128)(2,1)S(1)} %get-tuple-element.84), channel_id=1, source_target_pairs={{0,8},{8,0},{16,24},{24,16},{1,9},{9,1},{17,25},{25,17},{2,10},{10... | collective-permute-start | bytes 589832 | tf_op jit(solution)/shard_map/ppermute | solution.py:45
  83.9 30.1 %copy-start.1 = (f32[1,512,128]{2,1,0:T(8,128)S(1)}, f32[1,512,128]{2,1,0:T(8,128)}, u32[]{:S(2)}) copy-start(f32[1,512,128]{2,1,0:T(8,128)} %param.11) | copy-start | bytes 786436
  88.5 27.5 %collective-permute-start.26 = (bf16[512,256]{1,0:T(8,128)(2,1)S(1)}, bf16[512,256]{1,0:T(8,128)(2,1)S(1)}, u32[]{:S(2)}, u32[]{:S(2)}) collective-permute-start(bf16[512,256]{1,0:T(8,128)(2,1)S(1)} %get-tuple-element.99), channel_id=1, source_target_pairs={{0,8},{8,0},{16,24},{24,16},{1,9},{9,1},{17,25},{25,17},{2,10},{10... | collective-permute-start | bytes 786440 | tf_op jit(solution)/shard_map/ppermute | solution.py:45
  90.6 25.3 %collective-permute-start.27 = (bf16[512,256]{1,0:T(8,128)(2,1)S(1)}, bf16[512,256]{1,0:T(8,128)(2,1)S(1)}, u32[]{:S(2)}, u32[]{:S(2)}) collective-permute-start(bf16[512,256]{1,0:T(8,128)(2,1)S(1)} %get-tuple-element.100), channel_id=1, source_target_pairs={{0,16},{8,24},{16,0},{24,8},{1,17},{9,25},{17,1},{25,9},{2,18},{10... | collective-permute-start | bytes 786440 | tf_op jit(solution)/shard_map/ppermute | solution.py:45
  93.6 22.4 %collective-permute-start.28 = (bf16[512,256]{1,0:T(8,128)(2,1)S(1)}, bf16[512,256]{1,0:T(8,128)(2,1)S(1)}, u32[]{:S(2)}, u32[]{:S(2)}) collective-permute-start(bf16[512,256]{1,0:T(8,128)(2,1)S(1)} %get-tuple-element.101), channel_id=1, source_target_pairs={{0,24},{8,16},{16,8},{24,0},{1,25},{9,17},{17,9},{25,1},{2,26},{10... | collective-permute-start | bytes 786440 | tf_op jit(solution)/shard_map/ppermute | solution.py:45
  97.8 5.1 %collective-permute-start.23 = (f32[128,128]{1,0:T(8,128)S(1)}, f32[128,128]{1,0:T(8,128)S(1)}, u32[]{:S(2)}, u32[]{:S(2)}) collective-permute-start(f32[128,128]{1,0:T(8,128)S(1)} %get-tuple-element.92), channel_id=1, source_target_pairs={{0,1},{1,0},{2,3},{3,2},{4,5},{5,4},{6,7},{7,6},{8,9},{9,8},{10,11... | collective-permute-start | bytes 196616 | tf_op jit(solution)/shard_map/ppermute | solution.py:45
  103.0 5.5 %collective-permute-start.24 = (f32[128,128]{1,0:T(8,128)S(1)}, f32[128,128]{1,0:T(8,128)S(1)}, u32[]{:S(2)}, u32[]{:S(2)}) collective-permute-start(f32[128,128]{1,0:T(8,128)S(1)} %add.9), channel_id=1, source_target_pairs={{0,2},{1,3},{2,0},{3,1},{4,6},{5,7},{6,4},{7,5},{8,10},{9,11},{10,... | collective-permute-start | bytes 196616 | tf_op jit(solution)/shard_map/ppermute | solution.py:45
  108.5 5.6 %collective-permute-start.25 = (f32[128,128]{1,0:T(8,128)S(1)}, f32[128,128]{1,0:T(8,128)S(1)}, u32[]{:S(2)}, u32[]{:S(2)}) collective-permute-start(f32[128,128]{1,0:T(8,128)S(1)} %add.10), channel_id=1, source_target_pairs={{0,4},{1,5},{2,6},{3,7},{4,0},{5,1},{6,2},{7,3},{8,12},{9,13},{10,... | collective-permute-start | bytes 196616 | tf_op jit(solution)/shard_map/ppermute | solution.py:45
